TPU v7x, 32 devices: a whole 2x2x4 slice. The times are simulated.
32 devices in a mesh: grp: 2 (over x), row: 16 (over z, y, core).
Axes of the slice: x: 2, y: 2, z: 4, core: 2. Of those that a mesh axis runs over, the one named last changes fastest.
Arguments:
- system: float32 [32768, 16384], P(('grp', 'row')), parts along dimension 0, may hold values from -150 to 150
- measured: float32 [32768, 512], P(('grp', 'row')), parts along dimension 0, may hold values from -24 to 24
- row_class: int32 [32768], P(('grp', 'row')), parts along dimension 0, may hold values from 0 to 7
- band_weight: float32 [16], P('grp'), parts along dimension 0, may hold values from 0.3 to 1.5
- order: int32 [32, 2], P(('grp', 'row')), parts along dimension 0, may hold values from 0 to 1, each once within a row
Outputs:
- reconstruction: float32 [1024, 16384], P(('grp', 'row')), parts along dimension 0
There are 2 independent parts, one for each index of `grp`. A program takes and returns all parts, laid end to end along the dimension named above; each array names one. Nothing has to cross between parts.
All inputs are finite; a program needn't handle non-finite values.
Results may differ from a plain program's by a relative error of at most 0.0001.
Values sent between devices are 32-bit elements; how exact they have to be, the bound alone decides.
A program may use at most 128 MiB of HBM per device.

v0:
```python
import jax
import jax.numpy as jnp
from jax import lax
from jax.sharding import PartitionSpec as P

BATCH_FRAMES = 32
STEPS = 6


epsilon = 1e-06


def shifted(value, axis, steps):
    count = lax.axis_size(axis)
    pairs = [(source, (source + steps) % count) for source in range(count)]
    return lax.ppermute(value, axis, pairs)


def local(system, measured, row_class, band_weight, order):
    cycle_size = lax.axis_size("row")
    position = lax.axis_index("row")
    rows_here = system.shape[0]
    voxels = system.shape[1]
    subblocks = order.shape[1]
    subblock_rows = rows_here // subblocks
    band_hits = (
        row_class[:, None] == jnp.arange(band_weight.shape[0], dtype=jnp.int32)[None, :]
    ).astype(jnp.float32)
    row_weight = jnp.dot(band_hits, band_weight, precision=lax.Precision.HIGHEST) / (
        jnp.sum(system * system, axis=1) + epsilon
    )
    sequence = order[0]
    ordered = []
    for which in range(subblocks):
        first_row = sequence[which] * subblock_rows
        ordered.append(
            (
                lax.dynamic_slice_in_dim(system, first_row, subblock_rows, 0),
                lax.dynamic_slice_in_dim(row_weight, first_row, subblock_rows, 0),
                first_row,
            )
        )
    particle_image = jnp.zeros((BATCH_FRAMES, voxels), jnp.float32)
    for visit_no in range(STEPS):
        visit_particle_image = particle_image
        frame_count = visit_particle_image.shape[0]
        owner = (position - visit_no) % cycle_size
        first_frame = owner * BATCH_FRAMES
        for visit_which, (sub_matrix, sub_weight, visit_first_row) in enumerate(ordered):
            observed_signal = lax.dynamic_slice(
                measured, (visit_first_row, first_frame), (subblock_rows, frame_count)
            )
            if visit_no == 0 and visit_which == 0:
                residual = observed_signal.T
            else:
                forward = jnp.einsum(
                    "fv,rv->fr", visit_particle_image, sub_matrix, precision=lax.Precision.HIGHEST
                )
                residual = observed_signal.T - forward
            visit_particle_image = jnp.maximum(
                visit_particle_image
                + jnp.einsum(
                    "fr,rv->fv",
                    residual * sub_weight[None, :],
                    sub_matrix,
                    precision=lax.Precision.HIGHEST,
                ),
                0.0,
            )
        particle_image = visit_particle_image
        if visit_no + 1 < STEPS:
            particle_image = shifted(particle_image, "row", 1)
    return shifted(particle_image, "row", 1 - STEPS)


def solution(mesh):
    return jax.shard_map(
        local,
        mesh=mesh,
        in_specs=(
            P(("grp", "row"), None),
            P(("grp", "row"), None),
            P(("grp", "row")),
            P("grp"),
            P(("grp", "row"), None),
        ),
        out_specs=P(("grp", "row"), None),
        check_vma=False,
    )
```

profile of v0, /device:TPU:29, one launch (start us, length us, event | category | flops | bytes accessed | tf_op | source)
XLA Modules:
  0.0 881.2 jit_solution(18193908468026387981)
XLA Ops:
  47.2 30.3 %fusion.48 = f32[32,512]{0,1:T(8,128)S(1)} fusion(f32[32,16384]{1,0:T(8,128)S(1)} %convolution_maximum_fusion, f32[1024,16384]{1,0:T(8,128)} %param.5, s32[]{:T(128)S(6)} %select_n.74, f32[1024,512]{1,0:T(8,128)} %param.6, s32[]{:T(128)S(6)} %select_n.73, f32[512]{0:T(512)S(1)} %get-tuple-element.5), kind=kOutput, calls=%fused_computation.59 | convolution fusion | flops 3221258240 | bytes 35982848 | tf_op jit(solution)/shard_map/fv,rv->fr/dot_general | solution.py:56
  77.4 26.4 %fusion = f32[32,16384]{1,0:T(8,128)} fusion(f32[32,16384]{1,0:T(8,128)S(1)} %convolution_maximum_fusion, f32[32,512]{0,1:T(8,128)S(1)} %fusion.48, f32[1024,16384]{1,0:T(8,128)} %param.5, s32[]{:T(128)S(6)} %select_n.74), kind=kOutput, calls=%fused_computation.13 | convolution fusion | flops 3222274048 | bytes 37814276 | tf_op jit(solution)/shard_map/fr,rv->fv/dot_general | solution.py:62
  128.5 30.4 %fusion.84 = f32[32,512]{0,1:T(8,128)S(1)} fusion(f32[32,16384]{1,0:T(8,128)S(1)} %collective-permute-done, f32[1024,16384]{1,0:T(8,128)} %param.5, s32[]{:T(128)S(6)} %select_n.71, f32[1024,512]{1,0:T(8,128)} %param.6, s32[]{:T(128)S(6)} %select_n.76, f32[512]{0:T(512)S(1)} %get-tuple-element.6), kind=kOutput, calls=%fused_computation.71 | convolution fusion | flops 3221258240 | bytes 35982848 | tf_op jit(solution)/shard_map/fv,rv->fr/dot_general | solution.py:56
  158.9 25.4 %fusion.1 = f32[32,16384]{1,0:T(8,128)S(1)} fusion(f32[32,16384]{1,0:T(8,128)} %copy-done.2, f32[32,512]{0,1:T(8,128)S(1)} %fusion.84, f32[1024,16384]{1,0:T(8,128)} %param.5, s32[]{:T(128)S(6)} %select_n.71), kind=kOutput, calls=%fused_computation.14 | convolution fusion | flops 3222274048 | bytes 37814276 | tf_op jit(solution)/shard_map/fr,rv->fv/dot_general | solution.py:62
  184.3 30.5 %fusion.54 = f32[32,512]{0,1:T(8,128)S(1)} fusion(f32[32,16384]{1,0:T(8,128)S(1)} %fusion.1, f32[1024,16384]{1,0:T(8,128)} %param.5, s32[]{:T(128)S(6)} %select_n.74, f32[1024,512]{1,0:T(8,128)} %param.6, s32[]{:T(128)S(6)} %select_n.76, f32[512]{0:T(512)S(1)} %get-tuple-element.5), kind=kOutput, calls=%fused_computation.61 | convolution fusion | flops 3221258240 | bytes 35982848 | tf_op jit(solution)/shard_map/fv,rv->fr/dot_general | solution.py:56
  214.9 26.4 %fusion.2 = f32[32,16384]{1,0:T(8,128)} fusion(f32[32,16384]{1,0:T(8,128)S(1)} %fusion.1, f32[32,512]{0,1:T(8,128)S(1)} %fusion.54, f32[1024,16384]{1,0:T(8,128)} %param.5, s32[]{:T(128)S(6)} %select_n.74), kind=kOutput, calls=%fused_computation.15 | convolution fusion | flops 3222274048 | bytes 37814276 | tf_op jit(solution)/shard_map/fr,rv->fv/dot_general | solution.py:62
  246.4 23.3 %collective-permute-done.1 = f32[32,16384]{1,0:T(8,128)S(1)} collective-permute-done((f32[32,16384]{1,0:T(8,128)}, f32[32,16384]{1,0:T(8,128)S(1)}, u32[]{:S(2)}, u32[]{:S(2)}) %collective-permute-start.1) | collective-permute-done | bytes 2097184 | tf_op jit(solution)/shard_map/ppermute | solution.py:16
  271.0 30.4 %fusion.90 = f32[32,512]{0,1:T(8,128)S(1)} fusion(f32[32,16384]{1,0:T(8,128)S(1)} %collective-permute-done.1, f32[1024,16384]{1,0:T(8,128)} %param.5, s32[]{:T(128)S(6)} %select_n.71, f32[1024,512]{1,0:T(8,128)} %param.6, s32[]{:T(128)S(6)} %select_n.78, f32[512]{0:T(512)S(1)} %get-tuple-element.6), kind=kOutput, calls=%fused_computation.73 | convolution fusion | flops 3221258240 | bytes 35982848 | tf_op jit(solution)/shard_map/fv,rv->fr/dot_general | solution.py:56
  301.4 25.5 %fusion.3 = f32[32,16384]{1,0:T(8,128)S(1)} fusion(f32[32,16384]{1,0:T(8,128)} %copy-done.3, f32[32,512]{0,1:T(8,128)S(1)} %fusion.90, f32[1024,16384]{1,0:T(8,128)} %param.5, s32[]{:T(128)S(6)} %select_n.71), kind=kOutput, calls=%fused_computation.16 | convolution fusion | flops 3222274048 | bytes 37814276 | tf_op jit(solution)/shard_map/fr,rv->fv/dot_general | solution.py:62
  326.8 30.5 %fusion.60 = f32[32,512]{0,1:T(8,128)S(1)} fusion(f32[32,16384]{1,0:T(8,128)S(1)} %fusion.3, f32[1024,16384]{1,0:T(8,128)} %param.5, s32[]{:T(128)S(6)} %select_n.74, f32[1024,512]{1,0:T(8,128)} %param.6, s32[]{:T(128)S(6)} %select_n.78, f32[512]{0:T(512)S(1)} %get-tuple-element.5), kind=kOutput, calls=%fused_computation.63 | convolution fusion | flops 3221258240 | bytes 35982848 | tf_op jit(solution)/shard_map/fv,rv->fr/dot_general | solution.py:56
  357.3 26.4 %fusion.4 = f32[32,16384]{1,0:T(8,128)} fusion(f32[32,16384]{1,0:T(8,128)S(1)} %fusion.3, f32[32,512]{0,1:T(8,128)S(1)} %fusion.60, f32[1024,16384]{1,0:T(8,128)} %param.5, s32[]{:T(128)S(6)} %select_n.74), kind=kOutput, calls=%fused_computation.17 | convolution fusion | flops 3222274048 | bytes 37814276 | tf_op jit(solution)/shard_map/fr,rv->fv/dot_general | solution.py:62
  413.5 30.4 %fusion.96 = f32[32,512]{0,1:T(8,128)S(1)} fusion(f32[32,16384]{1,0:T(8,128)S(1)} %collective-permute-done.2, f32[1024,16384]{1,0:T(8,128)} %param.5, s32[]{:T(128)S(6)} %select_n.71, f32[1024,512]{1,0:T(8,128)} %param.6, s32[]{:T(128)S(6)} %select_n.80, f32[512]{0:T(512)S(1)} %get-tuple-element.6), kind=kOutput, calls=%fused_computation.75 | convolution fusion | flops 3221258240 | bytes 35982848 | tf_op jit(solution)/shard_map/fv,rv->fr/dot_general | solution.py:56
  443.8 25.5 %fusion.5 = f32[32,16384]{1,0:T(8,128)S(1)} fusion(f32[32,16384]{1,0:T(8,128)} %copy-done.4, f32[32,512]{0,1:T(8,128)S(1)} %fusion.96, f32[1024,16384]{1,0:T(8,128)} %param.5, s32[]{:T(128)S(6)} %select_n.71), kind=kOutput, calls=%fused_computation.18 | convolution fusion | flops 3222274048 | bytes 37814276 | tf_op jit(solution)/shard_map/fr,rv->fv/dot_general | solution.py:62
  469.3 30.5 %fusion.66 = f32[32,512]{0,1:T(8,128)S(1)} fusion(f32[32,16384]{1,0:T(8,128)S(1)} %fusion.5, f32[1024,16384]{1,0:T(8,128)} %param.5, s32[]{:T(128)S(6)} %select_n.74, f32[1024,512]{1,0:T(8,128)} %param.6, s32[]{:T(128)S(6)} %select_n.80, f32[512]{0:T(512)S(1)} %get-tuple-element.5), kind=kOutput, calls=%fused_computation.65 | convolution fusion | flops 3221258240 | bytes 35982848 | tf_op jit(solution)/shard_map/fv,rv->fr/dot_general | solution.py:56
  499.8 26.4 %fusion.6 = f32[32,16384]{1,0:T(8,128)} fusion(f32[32,16384]{1,0:T(8,128)S(1)} %fusion.5, f32[32,512]{0,1:T(8,128)S(1)} %fusion.66, f32[1024,16384]{1,0:T(8,128)} %param.5, s32[]{:T(128)S(6)} %select_n.74), kind=kOutput, calls=%fused_computation.19 | convolution fusion | flops 3222274048 | bytes 37814276 | tf_op jit(solution)/shard_map/fr,rv->fv/dot_general | solution.py:62
  555.9 30.4 %fusion.102 = f32[32,512]{0,1:T(8,128)S(1)} fusion(f32[32,16384]{1,0:T(8,128)S(1)} %collective-permute-done.3, f32[1024,16384]{1,0:T(8,128)} %param.5, s32[]{:T(128)S(6)} %select_n.71, f32[1024,512]{1,0:T(8,128)} %param.6, s32[]{:T(128)S(6)} %select_n.82, f32[512]{0:T(512)S(1)} %get-tuple-element.6), kind=kOutput, calls=%fused_computation.77 | convolution fusion | flops 3221258240 | bytes 35982848 | tf_op jit(solution)/shard_map/fv,rv->fr/dot_general | solution.py:56
  586.3 25.5 %fusion.7 = f32[32,16384]{1,0:T(8,128)S(1)} fusion(f32[32,16384]{1,0:T(8,128)} %copy-done.5, f32[32,512]{0,1:T(8,128)S(1)} %fusion.102, f32[1024,16384]{1,0:T(8,128)} %param.5, s32[]{:T(128)S(6)} %select_n.71), kind=kOutput, calls=%fused_computation.20 | convolution fusion | flops 3222274048 | bytes 37814276 | tf_op jit(solution)/shard_map/fr,rv->fv/dot_general | solution.py:62
  611.8 30.5 %fusion.72 = f32[32,512]{0,1:T(8,128)S(1)} fusion(f32[32,16384]{1,0:T(8,128)S(1)} %fusion.7, f32[1024,16384]{1,0:T(8,128)} %param.5, s32[]{:T(128)S(6)} %select_n.74, f32[1024,512]{1,0:T(8,128)} %param.6, s32[]{:T(128)S(6)} %select_n.82, f32[512]{0:T(512)S(1)} %get-tuple-element.5), kind=kOutput, calls=%fused_computation.67 | convolution fusion | flops 3221258240 | bytes 35982848 | tf_op jit(solution)/shard_map/fv,rv->fr/dot_general | solution.py:56
  642.3 26.4 %fusion.8 = f32[32,16384]{1,0:T(8,128)} fusion(f32[32,16384]{1,0:T(8,128)S(1)} %fusion.7, f32[32,512]{0,1:T(8,128)S(1)} %fusion.72, f32[1024,16384]{1,0:T(8,128)} %param.5, s32[]{:T(128)S(6)} %select_n.74), kind=kOutput, calls=%fused_computation.21 | convolution fusion | flops 3222274048 | bytes 37814276 | tf_op jit(solution)/shard_map/fr,rv->fv/dot_general | solution.py:62
  698.4 30.4 %fusion.108 = f32[32,512]{0,1:T(8,128)S(1)} fusion(f32[32,16384]{1,0:T(8,128)S(1)} %collective-permute-done.4, f32[1024,16384]{1,0:T(8,128)} %param.5, s32[]{:T(128)S(6)} %select_n.71, f32[1024,512]{1,0:T(8,128)} %param.6, s32[]{:T(128)S(6)} %select_n.84, f32[512]{0:T(512)S(1)} %get-tuple-element.6), kind=kOutput, calls=%fused_computation.79 | convolution fusion | flops 3221258240 | bytes 35982848 | tf_op jit(solution)/shard_map/fv,rv->fr/dot_general | solution.py:56
  728.8 25.5 %fusion.9 = f32[32,16384]{1,0:T(8,128)S(1)} fusion(f32[32,16384]{1,0:T(8,128)} %copy-done.1, f32[32,512]{0,1:T(8,128)S(1)} %fusion.108, f32[1024,16384]{1,0:T(8,128)} %param.5, s32[]{:T(128)S(6)} %select_n.71), kind=kOutput, calls=%fused_computation.22 | convolution fusion | flops 3222274048 | bytes 37814276 | tf_op jit(solution)/shard_map/fr,rv->fv/dot_general | solution.py:62
  754.3 30.5 %fusion.78 = f32[32,512]{0,1:T(8,128)S(1)} fusion(f32[32,16384]{1,0:T(8,128)S(1)} %fusion.9, f32[1024,16384]{1,0:T(8,128)} %param.5, s32[]{:T(128)S(6)} %select_n.74, f32[1024,512]{1,0:T(8,128)} %param.6, s32[]{:T(128)S(6)} %select_n.84, f32[512]{0:T(512)S(1)} %get-tuple-element.5), kind=kOutput, calls=%fused_computation.69 | convolution fusion | flops 3221258240 | bytes 35982848 | tf_op jit(solution)/shard_map/fv,rv->fr/dot_general | solution.py:56
  784.8 26.3 %fusion.10 = f32[32,16384]{1,0:T(8,128)} fusion(f32[32,16384]{1,0:T(8,128)S(1)} %fusion.9, f32[32,512]{0,1:T(8,128)S(1)} %fusion.78, f32[1024,16384]{1,0:T(8,128)} %param.5, s32[]{:T(128)S(6)} %select_n.74), kind=kOutput, calls=%fused_computation.23 | convolution fusion | flops 3222274048 | bytes 37814276 | tf_op jit(solution)/shard_map/fr,rv->fv/dot_general | solution.py:62
  811.0 68.4 %collective-permute-done.5 = f32[32,16384]{1,0:T(8,128)S(1)} collective-permute-done((f32[32,16384]{1,0:T(8,128)}, f32[32,16384]{1,0:T(8,128)S(1)}, u32[]{:S(2)}, u32[]{:S(2)}) %collective-permute-start.5) | collective-permute-done | bytes 2097184 | tf_op jit(solution)/shard_map/ppermute | solution.py:16
  (31 shorter events, 167.2 us)
Async XLA Ops:
  0.0 23.4 %copy-start = (f32[8]{0:T(128)S(1)}, f32[8]{0:T(128)}, u32[]{:S(2)}) copy-start(f32[8]{0:T(128)} %param.8) | copy-start | bytes 100
  2.6 20.8 %copy-start.6 = (s32[1024]{0:T(1024)S(1)}, s32[1024]{0:T(1024)}, u32[]{:S(2)}) copy-start(s32[1024]{0:T(1024)} %param.7) | copy-start | bytes 12292
  103.9 23.3 %collective-permute-start = (f32[32,16384]{1,0:T(8,128)}, f32[32,16384]{1,0:T(8,128)S(1)}, u32[]{:S(2)}, u32[]{:S(2)}) collective-permute-start(f32[32,16384]{1,0:T(8,128)} %fusion), channel_id=1, source_target_pairs={{0,1},{1,2},{2,3},{3,4},{4,5},{5,6},{6,7},{7,8},{8,9},{9,10},{10,1... | collective-permute-start | bytes 6291464 | tf_op jit(solution)/shard_map/ppermute | solution.py:16
  127.2 1.3 copy-start.2
  241.3 28.4 %collective-permute-start.1 = (f32[32,16384]{1,0:T(8,128)}, f32[32,16384]{1,0:T(8,128)S(1)}, u32[]{:S(2)}, u32[]{:S(2)}) collective-permute-start(f32[32,16384]{1,0:T(8,128)} %fusion.2), channel_id=1, source_target_pairs={{0,1},{1,2},{2,3},{3,4},{4,5},{5,6},{6,7},{7,8},{8,9},{9,10},{10,1... | collective-permute-start | bytes 6291464 | tf_op jit(solution)/shard_map/ppermute | solution.py:16
  269.7 1.3 copy-start.3
  383.8 28.4 %collective-permute-start.2 = (f32[32,16384]{1,0:T(8,128)}, f32[32,16384]{1,0:T(8,128)S(1)}, u32[]{:S(2)}, u32[]{:S(2)}) collective-permute-start(f32[32,16384]{1,0:T(8,128)} %fusion.4), channel_id=1, source_target_pairs={{0,1},{1,2},{2,3},{3,4},{4,5},{5,6},{6,7},{7,8},{8,9},{9,10},{10,1... | collective-permute-start | bytes 6291464 | tf_op jit(solution)/shard_map/ppermute | solution.py:16
  412.1 1.3 copy-start.4
  526.2 28.4 %collective-permute-start.3 = (f32[32,16384]{1,0:T(8,128)}, f32[32,16384]{1,0:T(8,128)S(1)}, u32[]{:S(2)}, u32[]{:S(2)}) collective-permute-start(f32[32,16384]{1,0:T(8,128)} %fusion.6), channel_id=1, source_target_pairs={{0,1},{1,2},{2,3},{3,4},{4,5},{5,6},{6,7},{7,8},{8,9},{9,10},{10,1... | collective-permute-start | bytes 6291464 | tf_op jit(solution)/shard_map/ppermute | solution.py:16
  554.6 1.3 copy-start.5
  668.7 28.4 %collective-permute-start.4 = (f32[32,16384]{1,0:T(8,128)}, f32[32,16384]{1,0:T(8,128)S(1)}, u32[]{:S(2)}, u32[]{:S(2)}) collective-permute-start(f32[32,16384]{1,0:T(8,128)} %fusion.8), channel_id=1, source_target_pairs={{0,1},{1,2},{2,3},{3,4},{4,5},{5,6},{6,7},{7,8},{8,9},{9,10},{10,1... | collective-permute-start | bytes 6291464 | tf_op jit(solution)/shard_map/ppermute | solution.py:16
  697.1 1.3 copy-start.1
  811.0 68.4 %collective-permute-start.5 = (f32[32,16384]{1,0:T(8,128)}, f32[32,16384]{1,0:T(8,128)S(1)}, u32[]{:S(2)}, u32[]{:S(2)}) collective-permute-start(f32[32,16384]{1,0:T(8,128)} %fusion.10), channel_id=1, source_target_pairs={{0,11},{1,12},{2,13},{3,14},{4,15},{5,0},{6,1},{7,2},{8,3},{9,4},{... | collective-permute-start | bytes 6291464 | tf_op jit(solution)/shard_map/ppermute | solution.py:16
where the time goes:
time: 890 us; the launch traced here: 881 us
  matrix products  644 us (72%)
  waiting for transfers between devices  185 us (21%)
  other arithmetic  20.8 us (2%)
  starting transfers between devices  20.3 us (2%)
  local copies, waits for them, and re-layouts  9.32 us (1%)
    dot_general x11, matrix products, local(): jnp.einsum('fv,rv->fr', visit_particle_image, sub_matrix, precision=lax.P...  335 us
    dot_general x12, matrix products, local(): jnp.einsum('fr,rv->fv', residual * sub_weight[None, :], sub_matrix, preci...  309 us
    ppermute x6, waiting for transfers between devices, shifted(): return lax.ppermute(value, axis, pairs)  185 us
    reduce_sum x1, other arithmetic, local(): jnp.sum(system * system, axis=1) + epsilon  20.8 us
    ppermute x6, starting transfers between devices, shifted(): return lax.ppermute(value, axis, pairs)  20.3 us
  transfers between devices with their start and end apart: 6, of which 6 were waited for; matrix products, arithmetic and copies ran while one was open for 0% of the time, Pallas kernels for 0%

commit v1 on v0

v1 whole, which is shorter than its diff:
```python
import functools

import jax
import jax.numpy as jnp
from jax import lax
from jax.experimental import pallas as pl
from jax.experimental.pallas import tpu as pltpu
from jax.sharding import PartitionSpec as P

BATCH_FRAMES = 32
STEPS = 6
TILE = 1024
PIECES = (4, 8, 4)
VMEM_BYTES = 40 * 1024 * 1024

epsilon = 1e-06


def two_parts(value):
    high = value.astype(jnp.bfloat16)
    low = (value - high.astype(jnp.float32)).astype(jnp.bfloat16)
    return high, low


def stacked_parts(image):
    high, low = two_parts(image)
    return jnp.concatenate([high, low, jnp.zeros((64, image.shape[1]), jnp.bfloat16)], axis=0)


def forward_product(matrix, parts):
    high, low = two_parts(matrix)
    dims = (((1,), (1,)), ((), ()))
    return lax.dot_general(
        high, parts, dims, preferred_element_type=jnp.float32
    ) + lax.dot_general(low, parts, dims, preferred_element_type=jnp.float32)


def update_product(weighted, matrix):
    high, low = two_parts(matrix)
    both = jnp.dot(weighted, high, preferred_element_type=jnp.float32)
    rest = jnp.dot(weighted[:BATCH_FRAMES], low, preferred_element_type=jnp.float32)
    return both[:BATCH_FRAMES] + both[BATCH_FRAMES:] + rest


def weighted_residual(signal, forward, weight):
    high, low = two_parts((signal - forward) * weight)
    return jnp.concatenate([high, low], axis=0)


def folded(total):
    turned = total.T
    return turned[:BATCH_FRAMES] + turned[BATCH_FRAMES : 2 * BATCH_FRAMES]


def first_kernel(scalars, signal, weight, weighted_out):
    weighted_out[...] = weighted_residual(signal[...], 0.0, weight[...])


def forward_kernel(first, last, *refs):
    refs = list(refs)[1:]
    matrix, image = refs[:2]
    rest = refs[2:]
    total_in = None if first else rest.pop(0)
    if last:
        signal, weight, out, total = rest
    else:
        (total,) = rest
    step = pl.program_id(0)

    @pl.when(step == 0)
    def _():
        total[...] = jnp.zeros_like(total) if first else total_in[...]

    total[...] += forward_product(matrix[...], stacked_parts(image[...]))

    if last:

        @pl.when(step == pl.num_programs(0) - 1)
        def _():
            out[...] = weighted_residual(signal[...], folded(total[...]), weight[...])


def middle_kernel(starts, *refs):
    refs = list(refs)[1:]
    old, new, weighted = refs[:3]
    pieces = refs[3 : 3 + len(starts)]
    signal, weight, image_out, weighted_out, total, parts = refs[3 + len(starts) :]
    step = pl.program_id(0)

    @pl.when(step == 0)
    def _():
        total[...] = jnp.zeros_like(total)
        parts[...] = jnp.zeros_like(parts)

    total[...] += forward_product(new[...], parts[...])
    change = update_product(weighted[...], old[...])
    if pieces:
        image = pieces[0][...]
        for start, piece in zip(starts[1:], pieces[1:]):
            image = jnp.where(step >= start, piece[...], image)
        change = image + change
    image = jnp.maximum(change, 0.0)
    image_out[...] = image
    parts[...] = stacked_parts(image)

    @pl.when(step == pl.num_programs(0) - 1)
    def _():
        weighted_out[...] = weighted_residual(signal[...], folded(total[...]), weight[...])


def last_kernel(scalars, matrix, weighted, image, *refs):
    image_out = refs[-1]
    image_out[...] = jnp.maximum(
        image[...] + update_product(weighted[...], matrix[...]), 0.0
    )


def called(kernel, grid, in_specs, out_specs, out_shape, scratch, flops, bytes_accessed):
    return pl.pallas_call(
        kernel,
        grid_spec=pltpu.PrefetchScalarGridSpec(
            num_scalar_prefetch=1,
            grid=(grid,),
            in_specs=in_specs,
            out_specs=out_specs,
            scratch_shapes=scratch,
        ),
        out_shape=out_shape,
        compiler_params=pltpu.CompilerParams(vmem_limit_bytes=VMEM_BYTES),
        cost_estimate=pl.CostEstimate(
            flops=flops, bytes_accessed=bytes_accessed, transcendentals=0
        ),
    )


def shifted(value, axis, steps):
    count = lax.axis_size(axis)
    pairs = [(source, (source + steps) % count) for source in range(count)]
    return lax.ppermute(value, axis, pairs)


def local(system, measured, row_class, band_weight, order):
    cycle_size = lax.axis_size("row")
    position = lax.axis_index("row")
    rows_here, voxels = system.shape
    rows = rows_here // order.shape[1]
    frames = BATCH_FRAMES
    tile = TILE
    tiles = voxels // tile
    counts = [share * tiles // sum(PIECES) for share in PIECES]
    starts = [sum(counts[:at]) for at in range(len(counts))]

    band_hits = (
        row_class[:, None] == jnp.arange(band_weight.shape[0], dtype=jnp.int32)[None, :]
    ).astype(jnp.float32)
    row_weight = jnp.dot(band_hits, band_weight, precision=lax.Precision.HIGHEST) / (
        jnp.sum(system * system, axis=1) + epsilon
    )
    row_weight = row_weight.reshape(-1, 1, rows)
    signals = measured.reshape(-1, rows, measured.shape[1]).transpose(0, 2, 1)

    f32, bf16 = jnp.float32, jnp.bfloat16
    weighted_shape = jax.ShapeDtypeStruct((2 * frames, rows), bf16)
    total_shape = jax.ShapeDtypeStruct((rows, 128), f32)
    total_scratch = pltpu.VMEM((rows, 128), f32)

    def matrix_spec(which, at):
        return pl.BlockSpec((rows, tile), lambda i, s: (s[which], at(i)))

    def signal_specs(which):
        return [
            pl.BlockSpec((None, frames, rows), lambda i, s: (s[which], s[2], 0)),
            pl.BlockSpec((None, 1, rows), lambda i, s: (s[which], 0, 0)),
        ]

    def whole_spec(shape):
        return pl.BlockSpec(shape, lambda i, s: (0, 0))

    weighted_spec = whole_spec((2 * frames, rows))
    total_spec = whole_spec((rows, 128))
    work = rows * tile
    moved = rows * tile // 4

    pieces = None
    for visit_no in range(STEPS):
        owner = (position - visit_no) % cycle_size
        scalars = jnp.stack([order[0, 0], order[0, 1], owner]).astype(jnp.int32)
        if pieces is None:
            weighted = called(
                first_kernel, 1, signal_specs(0), weighted_spec, weighted_shape, [], 1, 1
            )(scalars, signals, row_weight)
        else:
            total = None
            for at, (start, count) in enumerate(zip(starts, counts)):
                first, last = at == 0, at + 1 == len(counts)
                specs = [
                    matrix_spec(0, lambda i, start=start: start + i),
                    pl.BlockSpec((frames, tile), lambda i, s: (0, i)),
                ]
                values = [system, pieces[at]]
                if not first:
                    specs.append(total_spec)
                    values.append(total)
                if last:
                    specs += signal_specs(0)
                    values += [signals, row_weight]
                total = called(
                    functools.partial(forward_kernel, first, last),
                    count,
                    specs,
                    weighted_spec if last else total_spec,
                    weighted_shape if last else total_shape,
                    [total_scratch] if last else [],
                    work * count,
                    moved * count,
                )(scalars, *values)
            weighted = total

        inside = [] if pieces is None else pieces
        specs = [
            matrix_spec(0, lambda i: jnp.minimum(i, tiles - 1)),
            matrix_spec(1, lambda i: jnp.maximum(i - 1, 0)),
            weighted_spec,
        ]
        for start, count, _ in zip(starts, counts, inside):
            specs.append(
                pl.BlockSpec(
                    (frames, tile),
                    lambda i, s, start=start, count=count: (
                        0,
                        jnp.clip(i - start, 0, count - 1),
                    ),
                )
            )
        specs += signal_specs(1)
        image, weighted = called(
            functools.partial(middle_kernel, starts[: len(inside)]),
            tiles + 1,
            specs,
            [
                pl.BlockSpec((frames, tile), lambda i, s: (0, jnp.minimum(i, tiles - 1))),
                weighted_spec,
            ],
            [jax.ShapeDtypeStruct((frames, voxels), f32), weighted_shape],
            [total_scratch, pltpu.VMEM((128, tile), bf16)],
            2 * work * tiles,
            2 * moved * tiles,
        )(scalars, system, system, weighted, *inside, signals, row_weight)

        steps = 1 if visit_no + 1 < STEPS else 1 - STEPS
        pieces = []
        earlier = []
        for start, count in zip(starts, counts):
            piece = called(
                last_kernel,
                count,
                [
                    matrix_spec(1, lambda i, start=start: start + i),
                    weighted_spec,
                    pl.BlockSpec((frames, tile), lambda i, s, start=start: (0, start + i)),
                ]
                + [pl.BlockSpec(memory_space=pl.ANY)] * len(earlier),
                pl.BlockSpec((frames, tile), lambda i, s: (0, i)),
                jax.ShapeDtypeStruct((frames, count * tile), f32),
                [],
                work * count,
                moved * count,
            )(scalars, system, weighted, image, *earlier)
            earlier = [piece]
            pieces.append(shifted(piece, "row", steps))
    return jnp.concatenate(pieces, axis=1)


def solution(mesh):
    return jax.shard_map(
        local,
        mesh=mesh,
        in_specs=(
            P(("grp", "row"), None),
            P(("grp", "row"), None),
            P(("grp", "row")),
            P("grp"),
            P(("grp", "row"), None),
        ),
        out_specs=P(("grp", "row"), None),
        check_vma=False,
    )
```

time: 890 us -> 609 us (0.68)
  matrix products: 644 us -> 0.44 us
  Pallas kernels: 0 us -> 438 us
  waiting for transfers between devices: 185 us -> 112 us
  starting transfers between devices: 20.3 us -> 30.1 us
    dot_general x23 -> x0, matrix products: 644 us -> none  [the longest x11 335 us: local(): jnp.einsum('fv,rv->fr', visit_particle_image, sub_matrix, precision=lax.P...]
    pallas_call x0 -> x40, Pallas kernels: none -> 438 us  [the longest x6 190 us: local(): called(functools.partial(middle_kernel, starts[:len(inside)]), tiles + 1,...]
    ppermute x6 -> x18, waiting for transfers between devices: 185 us -> 112 us  [shifted(): return lax.ppermute(value, axis, pairs)]
    ppermute x6 -> x18, starting transfers between devices: 20.3 us -> 30.1 us  [shifted(): return lax.ppermute(value, axis, pairs)]
  transfers between devices with their start and end apart: 6 -> 18, of which waited for: 6 -> 7; matrix products, arithmetic and copies ran while one was open for 0% -> 0% of each run, Pallas kernels for 0% -> 20%
where the time goes in v1:
time: 609 us; the launch traced here: 607 us
  Pallas kernels  438 us (72%)
  waiting for transfers between devices  112 us (18%)
  starting transfers between devices  30.1 us (5%)
  other arithmetic  23.6 us (4%)
    pallas_call x6, Pallas kernels, local(): called(functools.partial(middle_kernel, starts[:len(inside)]), tiles + 1,...  190 us
    pallas_call x18, Pallas kernels, local(): called(last_kernel, count, [matrix_spec(1, lambda i, start=start: start +...  131 us
    pallas_call x15, Pallas kernels, local(): called(functools.partial(forward_kernel, first, last), count, specs, weig...  117 us
    ppermute x18, waiting for transfers between devices, shifted(): return lax.ppermute(value, axis, pairs)  112 us
    ppermute x18, starting transfers between devices, shifted(): return lax.ppermute(value, axis, pairs)  30.1 us
    reduce_sum x1, other arithmetic, local(): jnp.sum(system * system, axis=1) + epsilon  20.8 us
  transfers between devices with their start and end apart: 18, of which 7 were waited for; matrix products, arithmetic and copies ran while one was open for 0% of the time, Pallas kernels for 20%

profile of v1, /device:TPU:29, one launch (start us, length us, event | category | flops | bytes accessed | tf_op | source)
XLA Modules:
  0.0 607.3 jit_solution(7421555042462089080)
XLA Ops:
  3.3 20.8 %multiply_reduce_fusion = f32[1024]{0:T(1024)S(1)} fusion(f32[1024,16384]{1,0:T(8,128)} %matrix.35), kind=kLoop, calls=%fused_computation | loop fusion | flops 33553408 | bytes 67112960 | tf_op jit(solution)/shard_map/reduce_sum | solution.py:157
  26.5 31.4 %shard_map.56 = (f32[32,16384]{1,0:T(8,128)S(1)}, bf16[64,512]{1,0:T(8,128)(2,1)S(1)}) custom-call(s32[3]{0:T(128)S(1)} %get-tuple-element.29.scalars.refs_0_, f32[1024,16384]{1,0:T(8,128)} %matrix.35, f32[1024,16384]{1,0:T(8,128)} %matrix.35, bf16[64,512]{1,0:T(8,128)(2,1)S(1)} %shard_map.55.refs_3_, f32[2,512,512]{2,1,0:T(8,128)S(1)} %bitcast.16, ...), custom_call_target="tpu_custom_call" | custom-call | flops 16777216 | bytes 4194304 | tf_op jit(solution)/shard_map/pallas_call | solution.py:236
  64.2 11.0 %shard_map.58.refs_0_ = f32[32,8192]{1,0:T(8,128)} custom-call(s32[3]{0:T(128)S(1)} %get-tuple-element.29.scalars.refs_0_, f32[1024,16384]{1,0:T(8,128)} %matrix.35, bf16[64,512]{1,0:T(8,128)(2,1)S(1)} %get-tuple-element.17.weighted, f32[32,16384]{1,0:T(8,128)S(1)} %get-tuple-element.18.image, f32[32,4096]{1,0:T(8,128)} %shard_map.57.refs_0_), custom_call_target="tpu_custom_call" | custom-call | flops 4194304 | bytes 1048576 | tf_op jit(solution)/shard_map/pallas_call | solution.py:254
  83.7 9.2 %collective-permute-done.2.refs_2_.refs_4_ = f32[32,4096]{1,0:T(8,128)} collective-permute-done((f32[32,4096]{1,0:T(8,128)}, f32[32,4096]{1,0:T(8,128)}, u32[]{:S(2)}, u32[]{:S(2)}) %collective-permute-start.2) | collective-permute-done | bytes 524320 | tf_op jit(solution)/shard_map/ppermute | solution.py:139
  99.0 11.0 %shard_map.61.refs_3_ = f32[512,128]{1,0:T(8,128)S(1)} custom-call(s32[3]{0:T(128)S(1)} %get-tuple-element.31.refs_0_.scalars, f32[1024,16384]{1,0:T(8,128)} %matrix.35, f32[32,8192]{1,0:T(8,128)S(1)} %collective-permute-done.1.refs_2_.refs_5_, f32[512,128]{1,0:T(8,128)S(1)} %shard_map.60.refs_3_), custom_call_target="tpu_custom_call" | custom-call | flops 4194304 | bytes 1048576 | tf_op jit(solution)/shard_map/pallas_call | solution.py:207
  116.3 31.8 %shard_map.63 = (f32[32,16384]{1,0:T(8,128)S(1)}, bf16[64,512]{1,0:T(8,128)(2,1)S(1)}) custom-call(s32[3]{0:T(128)S(1)} %get-tuple-element.31.refs_0_.scalars, f32[1024,16384]{1,0:T(8,128)} %matrix.35, f32[1024,16384]{1,0:T(8,128)} %matrix.35, bf16[64,512]{1,0:T(8,128)(2,1)S(1)} %shard_map.62.refs_3_, f32[32,4096]{1,0:T(8,128)} %collective-permute-done.2.refs_2_.refs_4_, ...), custom_call_target="tpu_custom_call" | custom-call | flops 16777216 | bytes 4194304 | tf_op jit(solution)/shard_map/pallas_call | solution.py:236
  153.7 10.2 %shard_map.65.refs_0_ = f32[32,8192]{1,0:T(8,128)S(1)} custom-call(s32[3]{0:T(128)S(1)} %get-tuple-element.31.refs_0_.scalars, f32[1024,16384]{1,0:T(8,128)} %matrix.35, bf16[64,512]{1,0:T(8,128)(2,1)S(1)} %get-tuple-element.19.weighted, f32[32,16384]{1,0:T(8,128)S(1)} %get-tuple-element.20.image, f32[32,4096]{1,0:T(8,128)S(1)} %shard_map.64.refs_0_), custom_call_target="tpu_custom_call" | custom-call | flops 4194304 | bytes 1048576 | tf_op jit(solution)/shard_map/pallas_call | solution.py:254
  175.1 11.4 %collective-permute-done.5.refs_2_.refs_4_ = f32[32,4096]{1,0:T(8,128)S(1)} collective-permute-done((f32[32,4096]{1,0:T(8,128)S(1)}, f32[32,4096]{1,0:T(8,128)S(1)}, u32[]{:S(2)}, u32[]{:S(2)}) %collective-permute-start.5) | collective-permute-done | bytes 524320 | tf_op jit(solution)/shard_map/ppermute | solution.py:139
  192.6 11.0 %shard_map.68.refs_3_ = f32[512,128]{1,0:T(8,128)S(1)} custom-call(s32[3]{0:T(128)S(1)} %get-tuple-element.32.refs_0_.scalars, f32[1024,16384]{1,0:T(8,128)} %matrix.35, f32[32,8192]{1,0:T(8,128)S(1)} %collective-permute-done.4.refs_2_.refs_5_, f32[512,128]{1,0:T(8,128)S(1)} %shard_map.67.refs_3_), custom_call_target="tpu_custom_call" | custom-call | flops 4194304 | bytes 1048576 | tf_op jit(solution)/shard_map/pallas_call | solution.py:207
  209.9 31.7 %shard_map.70 = (f32[32,16384]{1,0:T(8,128)S(1)}, bf16[64,512]{1,0:T(8,128)(2,1)S(1)}) custom-call(s32[3]{0:T(128)S(1)} %get-tuple-element.32.refs_0_.scalars, f32[1024,16384]{1,0:T(8,128)} %matrix.35, f32[1024,16384]{1,0:T(8,128)} %matrix.35, bf16[64,512]{1,0:T(8,128)(2,1)S(1)} %shard_map.69.refs_3_, f32[32,4096]{1,0:T(8,128)S(1)} %collective-permute-done.5.refs_2_.refs_4_, ...), custom_call_target="tpu_custom_call" | custom-call | flops 16777216 | bytes 4194304 | tf_op jit(solution)/shard_map/pallas_call | solution.py:236
  247.2 10.2 %shard_map.72.refs_0_ = f32[32,8192]{1,0:T(8,128)S(1)} custom-call(s32[3]{0:T(128)S(1)} %get-tuple-element.32.refs_0_.scalars, f32[1024,16384]{1,0:T(8,128)} %matrix.35, bf16[64,512]{1,0:T(8,128)(2,1)S(1)} %get-tuple-element.21.weighted, f32[32,16384]{1,0:T(8,128)S(1)} %get-tuple-element.22.image, f32[32,4096]{1,0:T(8,128)S(1)} %shard_map.71.refs_0_), custom_call_target="tpu_custom_call" | custom-call | flops 4194304 | bytes 1048576 | tf_op jit(solution)/shard_map/pallas_call | solution.py:254
  268.5 11.6 %collective-permute-done.8.refs_2_.refs_4_ = f32[32,4096]{1,0:T(8,128)S(1)} collective-permute-done((f32[32,4096]{1,0:T(8,128)S(1)}, f32[32,4096]{1,0:T(8,128)S(1)}, u32[]{:S(2)}, u32[]{:S(2)}) %collective-permute-start.8) | collective-permute-done | bytes 524320 | tf_op jit(solution)/shard_map/ppermute | solution.py:139
  286.2 11.0 %shard_map.75.refs_3_ = f32[512,128]{1,0:T(8,128)S(1)} custom-call(s32[3]{0:T(128)S(1)} %get-tuple-element.33.refs_0_.scalars, f32[1024,16384]{1,0:T(8,128)} %matrix.35, f32[32,8192]{1,0:T(8,128)S(1)} %collective-permute-done.7.refs_2_.refs_5_, f32[512,128]{1,0:T(8,128)S(1)} %shard_map.74.refs_3_), custom_call_target="tpu_custom_call" | custom-call | flops 4194304 | bytes 1048576 | tf_op jit(solution)/shard_map/pallas_call | solution.py:207
  303.4 31.5 %shard_map.77 = (f32[32,16384]{1,0:T(8,128)S(1)}, bf16[64,512]{1,0:T(8,128)(2,1)S(1)}) custom-call(s32[3]{0:T(128)S(1)} %get-tuple-element.33.refs_0_.scalars, f32[1024,16384]{1,0:T(8,128)} %matrix.35, f32[1024,16384]{1,0:T(8,128)} %matrix.35, bf16[64,512]{1,0:T(8,128)(2,1)S(1)} %shard_map.76.refs_3_, f32[32,4096]{1,0:T(8,128)S(1)} %collective-permute-done.8.refs_2_.refs_4_, ...), custom_call_target="tpu_custom_call" | custom-call | flops 16777216 | bytes 4194304 | tf_op jit(solution)/shard_map/pallas_call | solution.py:236
  340.6 10.2 %shard_map.79.refs_0_ = f32[32,8192]{1,0:T(8,128)S(1)} custom-call(s32[3]{0:T(128)S(1)} %get-tuple-element.33.refs_0_.scalars, f32[1024,16384]{1,0:T(8,128)} %matrix.35, bf16[64,512]{1,0:T(8,128)(2,1)S(1)} %get-tuple-element.23.weighted, f32[32,16384]{1,0:T(8,128)S(1)} %get-tuple-element.24.image, f32[32,4096]{1,0:T(8,128)S(1)} %shard_map.78.refs_0_), custom_call_target="tpu_custom_call" | custom-call | flops 4194304 | bytes 1048576 | tf_op jit(solution)/shard_map/pallas_call | solution.py:254
  362.0 11.4 %collective-permute-done.11.refs_2_.refs_4_ = f32[32,4096]{1,0:T(8,128)S(1)} collective-permute-done((f32[32,4096]{1,0:T(8,128)S(1)}, f32[32,4096]{1,0:T(8,128)S(1)}, u32[]{:S(2)}, u32[]{:S(2)}) %collective-permute-start.11) | collective-permute-done | bytes 524320 | tf_op jit(solution)/shard_map/ppermute | solution.py:139
  379.4 11.0 %shard_map.82.refs_3_ = f32[512,128]{1,0:T(8,128)S(1)} custom-call(s32[3]{0:T(128)S(1)} %get-tuple-element.34.refs_0_.scalars, f32[1024,16384]{1,0:T(8,128)} %matrix.35, f32[32,8192]{1,0:T(8,128)S(1)} %collective-permute-done.10.refs_2_.refs_5_, f32[512,128]{1,0:T(8,128)S(1)} %shard_map.81.refs_3_), custom_call_target="tpu_custom_call" | custom-call | flops 4194304 | bytes 1048576 | tf_op jit(solution)/shard_map/pallas_call | solution.py:207
  396.7 31.7 %shard_map.84 = (f32[32,16384]{1,0:T(8,128)S(1)}, bf16[64,512]{1,0:T(8,128)(2,1)S(1)}) custom-call(s32[3]{0:T(128)S(1)} %get-tuple-element.34.refs_0_.scalars, f32[1024,16384]{1,0:T(8,128)} %matrix.35, f32[1024,16384]{1,0:T(8,128)} %matrix.35, bf16[64,512]{1,0:T(8,128)(2,1)S(1)} %shard_map.83.refs_3_, ...), custom_call_target="tpu_custom_call" | custom-call | flops 16777216 | bytes 4194304 | tf_op jit(solution)/shard_map/pallas_call | solution.py:236
  434.0 10.2 %shard_map.86.refs_0_ = f32[32,8192]{1,0:T(8,128)S(1)} custom-call(s32[3]{0:T(128)S(1)} %get-tuple-element.34.refs_0_.scalars, f32[1024,16384]{1,0:T(8,128)} %matrix.35, bf16[64,512]{1,0:T(8,128)(2,1)S(1)} %get-tuple-element.25.weighted, f32[32,16384]{1,0:T(8,128)S(1)} %get-tuple-element.26.image, f32[32,4096]{1,0:T(8,128)S(1)} %shard_map.85.refs_0_), custom_call_target="tpu_custom_call" | custom-call | flops 4194304 | bytes 1048576 | tf_op jit(solution)/shard_map/pallas_call | solution.py:254
  455.3 11.6 %collective-permute-done.14.refs_2_.refs_4_ = f32[32,4096]{1,0:T(8,128)S(1)} collective-permute-done((f32[32,4096]{1,0:T(8,128)S(1)}, f32[32,4096]{1,0:T(8,128)S(1)}, u32[]{:S(2)}, u32[]{:S(2)}) %collective-permute-start.14) | collective-permute-done | bytes 524320 | tf_op jit(solution)/shard_map/ppermute | solution.py:139
  473.0 11.0 %shard_map.89.refs_3_ = f32[512,128]{1,0:T(8,128)S(1)} custom-call(s32[3]{0:T(128)S(1)} %get-tuple-element.35.refs_0_.scalars, f32[1024,16384]{1,0:T(8,128)} %matrix.35, f32[32,8192]{1,0:T(8,128)S(1)} %collective-permute-done.13.refs_2_.refs_5_, f32[512,128]{1,0:T(8,128)S(1)} %shard_map.88.refs_3_), custom_call_target="tpu_custom_call" | custom-call | flops 4194304 | bytes 1048576 | tf_op jit(solution)/shard_map/pallas_call | solution.py:207
  490.2 31.5 %shard_map.91 = (f32[32,16384]{1,0:T(8,128)S(1)}, bf16[64,512]{1,0:T(8,128)(2,1)S(1)}) custom-call(s32[3]{0:T(128)S(1)} %get-tuple-element.35.refs_0_.scalars, f32[1024,16384]{1,0:T(8,128)} %matrix.35, f32[1024,16384]{1,0:T(8,128)} %matrix.35, bf16[64,512]{1,0:T(8,128)(2,1)S(1)} %shard_map.90.refs_3_, ...), custom_call_target="tpu_custom_call" | custom-call | flops 16777216 | bytes 4194304 | tf_op jit(solution)/shard_map/pallas_call | solution.py:236
  527.4 10.2 %shard_map.93.refs_0_ = f32[32,8192]{1,0:T(8,128)S(1)} custom-call(s32[3]{0:T(128)S(1)} %get-tuple-element.35.refs_0_.scalars, f32[1024,16384]{1,0:T(8,128)} %matrix.35, bf16[64,512]{1,0:T(8,128)(2,1)S(1)} %get-tuple-element.27.weighted, f32[32,16384]{1,0:T(8,128)S(1)} %get-tuple-element.28.image, f32[32,4096]{1,0:T(8,128)S(1)} %shard_map.92.refs_0_), custom_call_target="tpu_custom_call" | custom-call | flops 4194304 | bytes 1048576 | tf_op jit(solution)/shard_map/pallas_call | solution.py:254
  549.3 51.0 %collective-permute-done.17 = f32[32,4096]{1,0:T(8,128)S(1)} collective-permute-done((f32[32,4096]{1,0:T(8,128)S(1)}, f32[32,4096]{1,0:T(8,128)S(1)}, u32[]{:S(2)}, u32[]{:S(2)}) %collective-permute-start.17) | collective-permute-done | bytes 524320 | tf_op jit(solution)/shard_map/ppermute | solution.py:139
  (64 shorter events, 173.2 us)
Async XLA Ops:
  0.0 24.1 %copy-start = (f32[8]{0:T(128)S(1)}, f32[8]{0:T(128)}, u32[]{:S(2)}) copy-start(f32[8]{0:T(128)} %param.8) | copy-start | bytes 100
  3.3 20.8 %copy-start.1 = (s32[1024]{0:T(1024)S(1)}, s32[1024]{0:T(1024)}, u32[]{:S(2)}) copy-start(s32[1024]{0:T(1024)} %param.7) | copy-start | bytes 12292
  75.2 23.8 %collective-permute-start.1 = (f32[32,8192]{1,0:T(8,128)}, f32[32,8192]{1,0:T(8,128)S(1)}, u32[]{:S(2)}, u32[]{:S(2)}) collective-permute-start(f32[32,8192]{1,0:T(8,128)} %shard_map.58.refs_0_), channel_id=1, source_target_pairs={{0,1},{1,2},{2,3},{3,4},{4,5},{5,6},{6,7},{7,8},{8,9},{9,10},{10,1... | collective-permute-start | bytes 3145736 | tf_op jit(solution)/shard_map/ppermute | solution.py:139
  75.2 17.7 %collective-permute-start.2 = (f32[32,4096]{1,0:T(8,128)}, f32[32,4096]{1,0:T(8,128)}, u32[]{:S(2)}, u32[]{:S(2)}) collective-permute-start(f32[32,4096]{1,0:T(8,128)} %shard_map.57.refs_0_), channel_id=1, source_target_pairs={{0,1},{1,2},{2,3},{3,4},{4,5},{5,6},{6,7},{7,8},{8,9},{9,10},{10,1... | collective-permute-start | bytes 1572872 | tf_op jit(solution)/shard_map/ppermute | solution.py:139
  81.5 28.5 %collective-permute-start = (f32[32,4096]{1,0:T(8,128)}, f32[32,4096]{1,0:T(8,128)}, u32[]{:S(2)}, u32[]{:S(2)}) collective-permute-start(f32[32,4096]{1,0:T(8,128)} %shard_map.59), channel_id=1, source_target_pairs={{0,1},{1,2},{2,3},{3,4},{4,5},{5,6},{6,7},{7,8},{8,9},{9,10},{10,1... | collective-permute-start | bytes 1572872 | tf_op jit(solution)/shard_map/ppermute | solution.py:139
  163.9 28.7 %collective-permute-start.4 = (f32[32,8192]{1,0:T(8,128)S(1)}, f32[32,8192]{1,0:T(8,128)S(1)}, u32[]{:S(2)}, u32[]{:S(2)}) collective-permute-start(f32[32,8192]{1,0:T(8,128)S(1)} %shard_map.65.refs_0_), channel_id=1, source_target_pairs={{0,1},{1,2},{2,3},{3,4},{4,5},{5,6},{6,7},{7,8},{8,9},{9,10},{10,1... | collective-permute-start | bytes 3145736 | tf_op jit(solution)/shard_map/ppermute | solution.py:139
  169.2 17.4 %collective-permute-start.5 = (f32[32,4096]{1,0:T(8,128)S(1)}, f32[32,4096]{1,0:T(8,128)S(1)}, u32[]{:S(2)}, u32[]{:S(2)}) collective-permute-start(f32[32,4096]{1,0:T(8,128)S(1)} %shard_map.64.refs_0_), channel_id=1, source_target_pairs={{0,1},{1,2},{2,3},{3,4},{4,5},{5,6},{6,7},{7,8},{8,9},{9,10},{10,1... | collective-permute-start | bytes 1572872 | tf_op jit(solution)/shard_map/ppermute | solution.py:139
  174.9 28.8 %collective-permute-start.3 = (f32[32,4096]{1,0:T(8,128)S(1)}, f32[32,4096]{1,0:T(8,128)S(1)}, u32[]{:S(2)}, u32[]{:S(2)}) collective-permute-start(f32[32,4096]{1,0:T(8,128)S(1)} %shard_map.66), channel_id=1, source_target_pairs={{0,1},{1,2},{2,3},{3,4},{4,5},{5,6},{6,7},{7,8},{8,9},{9,10},{10,1... | collective-permute-start | bytes 1572872 | tf_op jit(solution)/shard_map/ppermute | solution.py:139
  257.5 28.7 %collective-permute-start.7 = (f32[32,8192]{1,0:T(8,128)S(1)}, f32[32,8192]{1,0:T(8,128)S(1)}, u32[]{:S(2)}, u32[]{:S(2)}) collective-permute-start(f32[32,8192]{1,0:T(8,128)S(1)} %shard_map.72.refs_0_), channel_id=1, source_target_pairs={{0,1},{1,2},{2,3},{3,4},{4,5},{5,6},{6,7},{7,8},{8,9},{9,10},{10,1... | collective-permute-start | bytes 3145736 | tf_op jit(solution)/shard_map/ppermute | solution.py:139
  262.7 17.4 %collective-permute-start.8 = (f32[32,4096]{1,0:T(8,128)S(1)}, f32[32,4096]{1,0:T(8,128)S(1)}, u32[]{:S(2)}, u32[]{:S(2)}) collective-permute-start(f32[32,4096]{1,0:T(8,128)S(1)} %shard_map.71.refs_0_), channel_id=1, source_target_pairs={{0,1},{1,2},{2,3},{3,4},{4,5},{5,6},{6,7},{7,8},{8,9},{9,10},{10,1... | collective-permute-start | bytes 1572872 | tf_op jit(solution)/shard_map/ppermute | solution.py:139
  268.4 28.8 %collective-permute-start.6 = (f32[32,4096]{1,0:T(8,128)S(1)}, f32[32,4096]{1,0:T(8,128)S(1)}, u32[]{:S(2)}, u32[]{:S(2)}) collective-permute-start(f32[32,4096]{1,0:T(8,128)S(1)} %shard_map.73), channel_id=1, source_target_pairs={{0,1},{1,2},{2,3},{3,4},{4,5},{5,6},{6,7},{7,8},{8,9},{9,10},{10,1... | collective-permute-start | bytes 1572872 | tf_op jit(solution)/shard_map/ppermute | solution.py:139
  350.7 28.7 %collective-permute-start.10 = (f32[32,8192]{1,0:T(8,128)S(1)}, f32[32,8192]{1,0:T(8,128)S(1)}, u32[]{:S(2)}, u32[]{:S(2)}) collective-permute-start(f32[32,8192]{1,0:T(8,128)S(1)} %shard_map.79.refs_0_), channel_id=1, source_target_pairs={{0,1},{1,2},{2,3},{3,4},{4,5},{5,6},{6,7},{7,8},{8,9},{9,10},{10,1... | collective-permute-start | bytes 3145736 | tf_op jit(solution)/shard_map/ppermute | solution.py:139
  356.0 17.4 %collective-permute-start.11 = (f32[32,4096]{1,0:T(8,128)S(1)}, f32[32,4096]{1,0:T(8,128)S(1)}, u32[]{:S(2)}, u32[]{:S(2)}) collective-permute-start(f32[32,4096]{1,0:T(8,128)S(1)} %shard_map.78.refs_0_), channel_id=1, source_target_pairs={{0,1},{1,2},{2,3},{3,4},{4,5},{5,6},{6,7},{7,8},{8,9},{9,10},{10,1... | collective-permute-start | bytes 1572872 | tf_op jit(solution)/shard_map/ppermute | solution.py:139
  361.7 28.8 %collective-permute-start.9 = (f32[32,4096]{1,0:T(8,128)S(1)}, f32[32,4096]{1,0:T(8,128)S(1)}, u32[]{:S(2)}, u32[]{:S(2)}) collective-permute-start(f32[32,4096]{1,0:T(8,128)S(1)} %shard_map.80), channel_id=1, source_target_pairs={{0,1},{1,2},{2,3},{3,4},{4,5},{5,6},{6,7},{7,8},{8,9},{9,10},{10,1... | collective-permute-start | bytes 1572872 | tf_op jit(solution)/shard_map/ppermute | solution.py:139
  444.3 28.7 %collective-permute-start.13 = (f32[32,8192]{1,0:T(8,128)S(1)}, f32[32,8192]{1,0:T(8,128)S(1)}, u32[]{:S(2)}, u32[]{:S(2)}) collective-permute-start(f32[32,8192]{1,0:T(8,128)S(1)} %shard_map.86.refs_0_), channel_id=1, source_target_pairs={{0,1},{1,2},{2,3},{3,4},{4,5},{5,6},{6,7},{7,8},{8,9},{9,10},{10,1... | collective-permute-start | bytes 3145736 | tf_op jit(solution)/shard_map/ppermute | solution.py:139
  449.5 17.4 %collective-permute-start.14 = (f32[32,4096]{1,0:T(8,128)S(1)}, f32[32,4096]{1,0:T(8,128)S(1)}, u32[]{:S(2)}, u32[]{:S(2)}) collective-permute-start(f32[32,4096]{1,0:T(8,128)S(1)} %shard_map.85.refs_0_), channel_id=1, source_target_pairs={{0,1},{1,2},{2,3},{3,4},{4,5},{5,6},{6,7},{7,8},{8,9},{9,10},{10,1... | collective-permute-start | bytes 1572872 | tf_op jit(solution)/shard_map/ppermute | solution.py:139
  455.2 28.8 %collective-permute-start.12 = (f32[32,4096]{1,0:T(8,128)S(1)}, f32[32,4096]{1,0:T(8,128)S(1)}, u32[]{:S(2)}, u32[]{:S(2)}) collective-permute-start(f32[32,4096]{1,0:T(8,128)S(1)} %shard_map.87), channel_id=1, source_target_pairs={{0,1},{1,2},{2,3},{3,4},{4,5},{5,6},{6,7},{7,8},{8,9},{9,10},{10,1... | collective-permute-start | bytes 1572872 | tf_op jit(solution)/shard_map/ppermute | solution.py:139
  537.5 68.4 %collective-permute-start.16 = (f32[32,8192]{1,0:T(8,128)S(1)}, f32[32,8192]{1,0:T(8,128)S(1)}, u32[]{:S(2)}, u32[]{:S(2)}) collective-permute-start(f32[32,8192]{1,0:T(8,128)S(1)} %shard_map.93.refs_0_), channel_id=1, source_target_pairs={{0,11},{1,12},{2,13},{3,14},{4,15},{5,0},{6,1},{7,2},{8,3},{9,4},{... | collective-permute-start | bytes 3145736 | tf_op jit(solution)/shard_map/ppermute | solution.py:139
  543.2 57.0 %collective-permute-start.17 = (f32[32,4096]{1,0:T(8,128)S(1)}, f32[32,4096]{1,0:T(8,128)S(1)}, u32[]{:S(2)}, u32[]{:S(2)}) collective-permute-start(f32[32,4096]{1,0:T(8,128)S(1)} %shard_map.94), channel_id=1, source_target_pairs={{0,11},{1,12},{2,13},{3,14},{4,15},{5,0},{6,1},{7,2},{8,3},{9,4},{... | collective-permute-start | bytes 1572872 | tf_op jit(solution)/shard_map/ppermute | solution.py:139
  543.3 62.6 %collective-permute-start.15 = (f32[32,4096]{1,0:T(8,128)S(1)}, f32[32,4096]{1,0:T(8,128)S(1)}, u32[]{:S(2)}, u32[]{:S(2)}) collective-permute-start(f32[32,4096]{1,0:T(8,128)S(1)} %shard_map.92.refs_0_), channel_id=1, source_target_pairs={{0,11},{1,12},{2,13},{3,14},{4,15},{5,0},{6,1},{7,2},{8,3},{9,4},{... | collective-permute-start | bytes 1572872 | tf_op jit(solution)/shard_map/ppermute | solution.py:139

commit v2 on v1

--- a/solution.py
+++ b/solution.py
@@ -10,7 +10,7 @@
 BATCH_FRAMES = 32
 STEPS = 6
 TILE = 1024
-PIECES = (4, 8, 4)
+PIECES = (5, 6, 5)
 VMEM_BYTES = 40 * 1024 * 1024
 
 epsilon = 1e-06
@@ -56,11 +56,9 @@
     weighted_out[...] = weighted_residual(signal[...], 0.0, weight[...])
 
 
-def forward_kernel(first, last, *refs):
-    refs = list(refs)[1:]
-    matrix, image = refs[:2]
-    rest = refs[2:]
-    total_in = None if first else rest.pop(0)
+def forward_kernel(last, *refs):
+    matrix, image, total_in = refs[1:4]
+    rest = refs[4:]
     if last:
         signal, weight, out, total = rest
     else:
@@ -69,7 +67,7 @@
 
     @pl.when(step == 0)
     def _():
-        total[...] = jnp.zeros_like(total) if first else total_in[...]
+        total[...] = total_in[...]
 
     total[...] += forward_product(matrix[...], stacked_parts(image[...]))
 
@@ -113,6 +111,15 @@
     image_out[...] = jnp.maximum(
         image[...] + update_product(weighted[...], matrix[...]), 0.0
     )
+
+
+def crossing_kernel(scalars, old, new, weighted, image, arrived, image_out, total):
+    @pl.when(pl.program_id(0) == 0)
+    def _():
+        total[...] = jnp.zeros_like(total)
+
+    total[...] += forward_product(new[...], stacked_parts(arrived[...]))
+    image_out[...] = jnp.maximum(image[...] + update_product(weighted[...], old[...]), 0.0)
 
 
 def called(kernel, grid, in_specs, out_specs, out_shape, scratch, flops, bytes_accessed):
@@ -148,6 +155,7 @@
     tile = TILE
     tiles = voxels // tile
     counts = [share * tiles // sum(PIECES) for share in PIECES]
+    assert counts[0] == counts[-1] and sum(counts) == tiles
     starts = [sum(counts[:at]) for at in range(len(counts))]
 
     band_hits = (
@@ -190,22 +198,20 @@
                 first_kernel, 1, signal_specs(0), weighted_spec, weighted_shape, [], 1, 1
             )(scalars, signals, row_weight)
         else:
-            total = None
-            for at, (start, count) in enumerate(zip(starts, counts)):
-                first, last = at == 0, at + 1 == len(counts)
+            for at in range(1, len(counts)):
+                start, count = starts[at], counts[at]
+                last = at + 1 == len(counts)
                 specs = [
                     matrix_spec(0, lambda i, start=start: start + i),
                     pl.BlockSpec((frames, tile), lambda i, s: (0, i)),
+                    total_spec,
                 ]
-                values = [system, pieces[at]]
-                if not first:
-                    specs.append(total_spec)
-                    values.append(total)
+                values = [system, pieces[at], total]
                 if last:
                     specs += signal_specs(0)
                     values += [signals, row_weight]
                 total = called(
-                    functools.partial(forward_kernel, first, last),
+                    functools.partial(forward_kernel, last),
                     count,
                     specs,
                     weighted_spec if last else total_spec,
@@ -250,7 +256,26 @@
         steps = 1 if visit_no + 1 < STEPS else 1 - STEPS
         pieces = []
         earlier = []
-        for start, count in zip(starts, counts):
+        for at, (start, count) in enumerate(zip(starts, counts)):
+            if at + 1 == len(counts) and visit_no + 1 < STEPS:
+                piece, total = called(
+                    crossing_kernel,
+                    count,
+                    [
+                        matrix_spec(1, lambda i, start=start: start + i),
+                        matrix_spec(0, lambda i: i),
+                        weighted_spec,
+                        pl.BlockSpec((frames, tile), lambda i, s, start=start: (0, start + i)),
+                        pl.BlockSpec((frames, tile), lambda i, s: (0, i)),
+                    ],
+                    [pl.BlockSpec((frames, tile), lambda i, s: (0, i)), total_spec],
+                    [jax.ShapeDtypeStruct((frames, count * tile), f32), total_shape],
+                    [],
+                    2 * work * count,
+                    2 * moved * count,
+                )(scalars, system, system, weighted, image, pieces[0])
+                pieces.append(shifted(piece, "row", steps))
+                continue
             piece = called(
                 last_kernel,
                 count,

time: 609 us -> 553 us (0.908)
  waiting for transfers between devices: 112 us -> 52.7 us
  starting transfers between devices: 30.1 us -> 44.7 us
  Pallas kernels: 438 us -> 424 us
    ppermute x18, waiting for transfers between devices: 112 us -> 52.7 us  [shifted(): return lax.ppermute(value, axis, pairs)]
    pallas_call x18 -> x13, Pallas kernels: 131 us -> 97.4 us  [local(): called(last_kernel, count, [matrix_spec(1, lambda i, start=start: start +...]
    pallas_call x15, Pallas kernels: 117 us -> 136 us  [the longest x10 81.1 us: local(): called(functools.partial(forward_kernel, last), count, specs, weighted_sp...]
    ppermute x18, starting transfers between devices: 30.1 us -> 44.7 us  [shifted(): return lax.ppermute(value, axis, pairs)]
  transfers between devices with their start and end apart: 18 -> 18, of which waited for: 7 -> 2; matrix products, arithmetic and copies ran while one was open for 0% -> 0% of each run, Pallas kernels for 20% -> 26%
where the time goes in v2:
time: 553 us; the launch traced here: 551 us
  Pallas kernels  424 us (77%)
  waiting for transfers between devices  52.7 us (10%)
  starting transfers between devices  44.7 us (8%)
  other arithmetic  23.6 us (4%)
    pallas_call x6, Pallas kernels, local(): called(functools.partial(middle_kernel, starts[:len(inside)]), tiles + 1,...  190 us
    pallas_call x13, Pallas kernels, local(): called(last_kernel, count, [matrix_spec(1, lambda i, start=start: start +...  97.4 us
    pallas_call x10, Pallas kernels, local(): called(functools.partial(forward_kernel, last), count, specs, weighted_sp...  81.1 us
    pallas_call x5, Pallas kernels, local(): called(crossing_kernel, count, [matrix_spec(1, lambda i, start=start: sta...  54.8 us
    ppermute x18, waiting for transfers between devices, shifted(): return lax.ppermute(value, axis, pairs)  52.7 us
    ppermute x18, starting transfers between devices, shifted(): return lax.ppermute(value, axis, pairs)  44.7 us
    reduce_sum x1, other arithmetic, local(): jnp.sum(system * system, axis=1) + epsilon  20.8 us
  transfers between devices with their start and end apart: 18, of which 2 were waited for; matrix products, arithmetic and copies ran while one was open for 0% of the time, Pallas kernels for 26%

profile of v2, /device:TPU:29, one launch (start us, length us, event | category | flops | bytes accessed | tf_op | source)
XLA Modules:
  0.0 550.5 jit_solution(9515677847238302134)
XLA Ops:
  3.3 20.8 %multiply_reduce_fusion = f32[1024]{0:T(1024)S(1)} fusion(f32[1024,16384]{1,0:T(8,128)} %matrix.25), kind=kLoop, calls=%fused_computation | loop fusion | flops 33553408 | bytes 67112960 | tf_op jit(solution)/shard_map/reduce_sum | solution.py:165
  26.5 31.4 %shard_map.56 = (f32[32,16384]{1,0:T(8,128)S(1)}, bf16[64,512]{1,0:T(8,128)(2,1)S(1)}) custom-call(s32[3]{0:T(128)S(1)} %get-tuple-element.49.scalars.refs_0_, f32[1024,16384]{1,0:T(8,128)} %matrix.25, f32[1024,16384]{1,0:T(8,128)} %matrix.25, bf16[64,512]{1,0:T(8,128)(2,1)S(1)} %shard_map.55.refs_3_, f32[2,512,512]{2,1,0:T(8,128)S(1)} %bitcast.16, ...), custom_call_target="tpu_custom_call" | custom-call | flops 16777216 | bytes 4194304 | tf_op jit(solution)/shard_map/pallas_call | solution.py:242
  65.0 8.6 %shard_map.59 = f32[32,6144]{1,0:T(8,128)} custom-call(s32[3]{0:T(128)S(1)} %get-tuple-element.49.scalars.refs_0_, f32[1024,16384]{1,0:T(8,128)} %matrix.25, bf16[64,512]{1,0:T(8,128)(2,1)S(1)} %get-tuple-element.27.weighted, f32[32,16384]{1,0:T(8,128)S(1)} %get-tuple-element.28.image, f32[32,5120]{1,0:T(8,128)S(1)} %shard_map.57.refs_0_), custom_call_target="tpu_custom_call" | custom-call | flops 3145728 | bytes 786432 | tf_op jit(solution)/shard_map/pallas_call | solution.py:279
  73.7 11.5 %shard_map.58 = (f32[32,5120]{1,0:T(8,128)}, f32[512,128]{1,0:T(8,128)S(1)}) custom-call(s32[3]{0:T(128)S(1)} %get-tuple-element.49.scalars.refs_0_, f32[1024,16384]{1,0:T(8,128)} %matrix.25, f32[1024,16384]{1,0:T(8,128)} %matrix.25, bf16[64,512]{1,0:T(8,128)(2,1)S(1)} %get-tuple-element.27.weighted, f32[32,16384]{1,0:T(8,128)S(1)} %get-tuple-element.28.image, ...), custom_call_target="tpu_custom_call" | custom-call | flops 5242880 | bytes 1310720 | tf_op jit(solution)/shard_map/pallas_call | solution.py:261
  91.0 8.6 %shard_map.60.refs_3_ = f32[512,128]{1,0:T(8,128)S(1)} custom-call(s32[3]{0:T(128)S(1)} %get-tuple-element.51.refs_0_.scalars, f32[1024,16384]{1,0:T(8,128)} %matrix.25, f32[32,6144]{1,0:T(8,128)S(1)} %collective-permute-done.2.refs_2_.refs_5_, f32[512,128]{1,0:T(8,128)S(1)} %copy-done.4), custom_call_target="tpu_custom_call" | custom-call | flops 3145728 | bytes 786432 | tf_op jit(solution)/shard_map/pallas_call | solution.py:213
  107.3 31.7 %shard_map.62 = (f32[32,16384]{1,0:T(8,128)S(1)}, bf16[64,512]{1,0:T(8,128)(2,1)S(1)}) custom-call(s32[3]{0:T(128)S(1)} %get-tuple-element.51.refs_0_.scalars, f32[1024,16384]{1,0:T(8,128)} %matrix.25, f32[1024,16384]{1,0:T(8,128)} %matrix.25, bf16[64,512]{1,0:T(8,128)(2,1)S(1)} %shard_map.61.refs_3_, f32[32,5120]{1,0:T(8,128)S(1)} %copy-done.2, ...), custom_call_target="tpu_custom_call" | custom-call | flops 16777216 | bytes 4194304 | tf_op jit(solution)/shard_map/pallas_call | solution.py:242
  149.4 7.9 %shard_map.65 = f32[32,6144]{1,0:T(8,128)S(1)} custom-call(s32[3]{0:T(128)S(1)} %get-tuple-element.51.refs_0_.scalars, f32[1024,16384]{1,0:T(8,128)} %matrix.25, bf16[64,512]{1,0:T(8,128)(2,1)S(1)} %get-tuple-element.31.weighted, f32[32,16384]{1,0:T(8,128)S(1)} %get-tuple-element.32.image, f32[32,5120]{1,0:T(8,128)S(1)} %shard_map.63.refs_0_), custom_call_target="tpu_custom_call" | custom-call | flops 3145728 | bytes 786432 | tf_op jit(solution)/shard_map/pallas_call | solution.py:279
  157.4 10.8 %shard_map.64 = (f32[32,5120]{1,0:T(8,128)S(1)}, f32[512,128]{1,0:T(8,128)S(1)}) custom-call(s32[3]{0:T(128)S(1)} %get-tuple-element.51.refs_0_.scalars, f32[1024,16384]{1,0:T(8,128)} %matrix.25, f32[1024,16384]{1,0:T(8,128)} %matrix.25, bf16[64,512]{1,0:T(8,128)(2,1)S(1)} %get-tuple-element.31.weighted, f32[32,16384]{1,0:T(8,128)S(1)} %get-tuple-element.32.image, ...), custom_call_target="tpu_custom_call" | custom-call | flops 5242880 | bytes 1310720 | tf_op jit(solution)/shard_map/pallas_call | solution.py:261
  173.1 8.6 %shard_map.66.refs_3_ = f32[512,128]{1,0:T(8,128)S(1)} custom-call(s32[3]{0:T(128)S(1)} %get-tuple-element.52.refs_0_.scalars, f32[1024,16384]{1,0:T(8,128)} %matrix.25, f32[32,6144]{1,0:T(8,128)S(1)} %collective-permute-done.5.refs_2_.refs_5_, f32[512,128]{1,0:T(8,128)S(1)} %get-tuple-element.34.refs_3_), custom_call_target="tpu_custom_call" | custom-call | flops 3145728 | bytes 786432 | tf_op jit(solution)/shard_map/pallas_call | solution.py:213
  189.4 31.7 %shard_map.68 = (f32[32,16384]{1,0:T(8,128)S(1)}, bf16[64,512]{1,0:T(8,128)(2,1)S(1)}) custom-call(s32[3]{0:T(128)S(1)} %get-tuple-element.52.refs_0_.scalars, f32[1024,16384]{1,0:T(8,128)} %matrix.25, f32[1024,16384]{1,0:T(8,128)} %matrix.25, bf16[64,512]{1,0:T(8,128)(2,1)S(1)} %shard_map.67.refs_3_, f32[32,5120]{1,0:T(8,128)S(1)} %collective-permute-done.3.arrived.refs_4_, ...), custom_call_target="tpu_custom_call" | custom-call | flops 16777216 | bytes 4194304 | tf_op jit(solution)/shard_map/pallas_call | solution.py:242
  232.3 7.9 %shard_map.71 = f32[32,6144]{1,0:T(8,128)S(1)} custom-call(s32[3]{0:T(128)S(1)} %get-tuple-element.52.refs_0_.scalars, f32[1024,16384]{1,0:T(8,128)} %matrix.25, bf16[64,512]{1,0:T(8,128)(2,1)S(1)} %get-tuple-element.35.weighted, f32[32,16384]{1,0:T(8,128)S(1)} %get-tuple-element.36.image, f32[32,5120]{1,0:T(8,128)S(1)} %shard_map.69.refs_0_), custom_call_target="tpu_custom_call" | custom-call | flops 3145728 | bytes 786432 | tf_op jit(solution)/shard_map/pallas_call | solution.py:279
  240.3 10.8 %shard_map.70 = (f32[32,5120]{1,0:T(8,128)S(1)}, f32[512,128]{1,0:T(8,128)S(1)}) custom-call(s32[3]{0:T(128)S(1)} %get-tuple-element.52.refs_0_.scalars, f32[1024,16384]{1,0:T(8,128)} %matrix.25, f32[1024,16384]{1,0:T(8,128)} %matrix.25, bf16[64,512]{1,0:T(8,128)(2,1)S(1)} %get-tuple-element.35.weighted, f32[32,16384]{1,0:T(8,128)S(1)} %get-tuple-element.36.image, ...), custom_call_target="tpu_custom_call" | custom-call | flops 5242880 | bytes 1310720 | tf_op jit(solution)/shard_map/pallas_call | solution.py:261
  255.9 8.6 %shard_map.72.refs_3_ = f32[512,128]{1,0:T(8,128)S(1)} custom-call(s32[3]{0:T(128)S(1)} %get-tuple-element.53.refs_0_.scalars, f32[1024,16384]{1,0:T(8,128)} %matrix.25, f32[32,6144]{1,0:T(8,128)S(1)} %collective-permute-done.8.refs_2_.refs_5_, f32[512,128]{1,0:T(8,128)S(1)} %get-tuple-element.38.refs_3_), custom_call_target="tpu_custom_call" | custom-call | flops 3145728 | bytes 786432 | tf_op jit(solution)/shard_map/pallas_call | solution.py:213
  272.1 31.5 %shard_map.74 = (f32[32,16384]{1,0:T(8,128)S(1)}, bf16[64,512]{1,0:T(8,128)(2,1)S(1)}) custom-call(s32[3]{0:T(128)S(1)} %get-tuple-element.53.refs_0_.scalars, f32[1024,16384]{1,0:T(8,128)} %matrix.25, f32[1024,16384]{1,0:T(8,128)} %matrix.25, bf16[64,512]{1,0:T(8,128)(2,1)S(1)} %shard_map.73.refs_3_, f32[32,5120]{1,0:T(8,128)S(1)} %collective-permute-done.6.arrived.refs_4_, ...), custom_call_target="tpu_custom_call" | custom-call | flops 16777216 | bytes 4194304 | tf_op jit(solution)/shard_map/pallas_call | solution.py:242
  314.9 7.9 %shard_map.77 = f32[32,6144]{1,0:T(8,128)S(1)} custom-call(s32[3]{0:T(128)S(1)} %get-tuple-element.53.refs_0_.scalars, f32[1024,16384]{1,0:T(8,128)} %matrix.25, bf16[64,512]{1,0:T(8,128)(2,1)S(1)} %get-tuple-element.39.weighted, f32[32,16384]{1,0:T(8,128)S(1)} %get-tuple-element.40.image, f32[32,5120]{1,0:T(8,128)S(1)} %shard_map.75.refs_0_), custom_call_target="tpu_custom_call" | custom-call | flops 3145728 | bytes 786432 | tf_op jit(solution)/shard_map/pallas_call | solution.py:279
  322.8 10.8 %shard_map.76 = (f32[32,5120]{1,0:T(8,128)S(1)}, f32[512,128]{1,0:T(8,128)S(1)}) custom-call(s32[3]{0:T(128)S(1)} %get-tuple-element.53.refs_0_.scalars, f32[1024,16384]{1,0:T(8,128)} %matrix.25, f32[1024,16384]{1,0:T(8,128)} %matrix.25, bf16[64,512]{1,0:T(8,128)(2,1)S(1)} %get-tuple-element.39.weighted, f32[32,16384]{1,0:T(8,128)S(1)} %get-tuple-element.40.image, ...), custom_call_target="tpu_custom_call" | custom-call | flops 5242880 | bytes 1310720 | tf_op jit(solution)/shard_map/pallas_call | solution.py:261
  338.6 8.5 %shard_map.78.refs_3_ = f32[512,128]{1,0:T(8,128)S(1)} custom-call(s32[3]{0:T(128)S(1)} %get-tuple-element.54.refs_0_.scalars, f32[1024,16384]{1,0:T(8,128)} %matrix.25, f32[32,6144]{1,0:T(8,128)S(1)} %collective-permute-done.11.refs_2_.refs_5_, f32[512,128]{1,0:T(8,128)S(1)} %get-tuple-element.42.refs_3_), custom_call_target="tpu_custom_call" | custom-call | flops 3145728 | bytes 786432 | tf_op jit(solution)/shard_map/pallas_call | solution.py:213
  354.9 31.7 %shard_map.80 = (f32[32,16384]{1,0:T(8,128)S(1)}, bf16[64,512]{1,0:T(8,128)(2,1)S(1)}) custom-call(s32[3]{0:T(128)S(1)} %get-tuple-element.54.refs_0_.scalars, f32[1024,16384]{1,0:T(8,128)} %matrix.25, f32[1024,16384]{1,0:T(8,128)} %matrix.25, bf16[64,512]{1,0:T(8,128)(2,1)S(1)} %shard_map.79.refs_3_, f32[32,5120]{1,0:T(8,128)S(1)} %collective-permute-done.9.arrived.refs_4_, ...), custom_call_target="tpu_custom_call" | custom-call | flops 16777216 | bytes 4194304 | tf_op jit(solution)/shard_map/pallas_call | solution.py:242
  397.8 7.9 %shard_map.83 = f32[32,6144]{1,0:T(8,128)S(1)} custom-call(s32[3]{0:T(128)S(1)} %get-tuple-element.54.refs_0_.scalars, f32[1024,16384]{1,0:T(8,128)} %matrix.25, bf16[64,512]{1,0:T(8,128)(2,1)S(1)} %get-tuple-element.43.weighted, f32[32,16384]{1,0:T(8,128)S(1)} %get-tuple-element.44.image, f32[32,5120]{1,0:T(8,128)S(1)} %shard_map.81.refs_0_), custom_call_target="tpu_custom_call" | custom-call | flops 3145728 | bytes 786432 | tf_op jit(solution)/shard_map/pallas_call | solution.py:279
  405.9 10.8 %shard_map.82 = (f32[32,5120]{1,0:T(8,128)S(1)}, f32[512,128]{1,0:T(8,128)S(1)}) custom-call(s32[3]{0:T(128)S(1)} %get-tuple-element.54.refs_0_.scalars, f32[1024,16384]{1,0:T(8,128)} %matrix.25, f32[1024,16384]{1,0:T(8,128)} %matrix.25, bf16[64,512]{1,0:T(8,128)(2,1)S(1)} %get-tuple-element.43.weighted, f32[32,16384]{1,0:T(8,128)S(1)} %get-tuple-element.44.image, ...), custom_call_target="tpu_custom_call" | custom-call | flops 5242880 | bytes 1310720 | tf_op jit(solution)/shard_map/pallas_call | solution.py:261
  421.4 8.6 %shard_map.84.refs_3_ = f32[512,128]{1,0:T(8,128)S(1)} custom-call(s32[3]{0:T(128)S(1)} %get-tuple-element.55.refs_0_.scalars, f32[1024,16384]{1,0:T(8,128)} %matrix.25, f32[32,6144]{1,0:T(8,128)S(1)} %collective-permute-done.14.refs_2_.refs_5_, f32[512,128]{1,0:T(8,128)S(1)} %get-tuple-element.46.refs_3_), custom_call_target="tpu_custom_call" | custom-call | flops 3145728 | bytes 786432 | tf_op jit(solution)/shard_map/pallas_call | solution.py:213
  437.7 31.7 %shard_map.86 = (f32[32,16384]{1,0:T(8,128)S(1)}, bf16[64,512]{1,0:T(8,128)(2,1)S(1)}) custom-call(s32[3]{0:T(128)S(1)} %get-tuple-element.55.refs_0_.scalars, f32[1024,16384]{1,0:T(8,128)} %matrix.25, f32[1024,16384]{1,0:T(8,128)} %matrix.25, bf16[64,512]{1,0:T(8,128)(2,1)S(1)} %shard_map.85.refs_3_, ...), custom_call_target="tpu_custom_call" | custom-call | flops 16777216 | bytes 4194304 | tf_op jit(solution)/shard_map/pallas_call | solution.py:242
  476.4 7.9 %shard_map.88.refs_0_ = f32[32,6144]{1,0:T(8,128)S(1)} custom-call(s32[3]{0:T(128)S(1)} %get-tuple-element.55.refs_0_.scalars, f32[1024,16384]{1,0:T(8,128)} %matrix.25, bf16[64,512]{1,0:T(8,128)(2,1)S(1)} %get-tuple-element.47.weighted, f32[32,16384]{1,0:T(8,128)S(1)} %get-tuple-element.48.image, f32[32,5120]{1,0:T(8,128)S(1)} %shard_map.87.refs_0_), custom_call_target="tpu_custom_call" | custom-call | flops 3145728 | bytes 786432 | tf_op jit(solution)/shard_map/pallas_call | solution.py:279
  496.4 45.7 %collective-permute-done.17 = f32[32,5120]{1,0:T(8,128)S(1)} collective-permute-done((f32[32,5120]{1,0:T(8,128)S(1)}, f32[32,5120]{1,0:T(8,128)S(1)}, u32[]{:S(2)}, u32[]{:S(2)}) %collective-permute-start.17) | collective-permute-done | bytes 655392 | tf_op jit(solution)/shard_map/ppermute | solution.py:146
  (67 shorter events, 148.1 us)
Async XLA Ops:
  0.0 24.1 %copy-start = (f32[8]{0:T(128)S(1)}, f32[8]{0:T(128)}, u32[]{:S(2)}) copy-start(f32[8]{0:T(128)} %param.8) | copy-start | bytes 100
  3.3 20.8 %copy-start.5 = (s32[1024]{0:T(1024)S(1)}, s32[1024]{0:T(1024)}, u32[]{:S(2)}) copy-start(s32[1024]{0:T(1024)} %param.7) | copy-start | bytes 12292
  65.0 8.7 %collective-permute-start = (f32[32,5120]{1,0:T(8,128)S(1)}, f32[32,5120]{1,0:T(8,128)S(1)}, u32[]{:S(2)}, u32[]{:S(2)}) collective-permute-start(f32[32,5120]{1,0:T(8,128)S(1)} %shard_map.57.refs_0_), channel_id=1, source_target_pairs={{0,1},{1,2},{2,3},{3,4},{4,5},{5,6},{6,7},{7,8},{8,9},{9,10},{10,1... | collective-permute-start | bytes 1966088 | tf_op jit(solution)/shard_map/ppermute | solution.py:146
  73.7 16.4 %collective-permute-start.2 = (f32[32,6144]{1,0:T(8,128)}, f32[32,6144]{1,0:T(8,128)S(1)}, u32[]{:S(2)}, u32[]{:S(2)}) collective-permute-start(f32[32,6144]{1,0:T(8,128)} %shard_map.59), channel_id=1, source_target_pairs={{0,1},{1,2},{2,3},{3,4},{4,5},{5,6},{6,7},{7,8},{8,9},{9,10},{10,1... | collective-permute-start | bytes 2359304 | tf_op jit(solution)/shard_map/ppermute | solution.py:146
  73.7 11.5 %copy-start.1 = (f32[32,5120]{1,0:T(8,128)}, f32[32,5120]{1,0:T(8,128)S(1)}, u32[]{:S(2)}) copy-start(f32[32,5120]{1,0:T(8,128)S(1)} %collective-permute-done.arrived.refs_4_) | copy-start | bytes 1966084
  85.2 0.7 copy-start.3
  85.9 13.6 %collective-permute-start.1 = (f32[32,5120]{1,0:T(8,128)}, f32[32,5120]{1,0:T(8,128)S(1)}, u32[]{:S(2)}, u32[]{:S(2)}) collective-permute-start(f32[32,5120]{1,0:T(8,128)} %get-tuple-element.29), channel_id=1, source_target_pairs={{0,1},{1,2},{2,3},{3,4},{4,5},{5,6},{6,7},{7,8},{8,9},{9,10},{10,1... | collective-permute-start | bytes 1966088 | tf_op jit(solution)/shard_map/ppermute | solution.py:146
  90.0 1.0 copy-start.4
  99.6 7.7 %copy-start.2 = (f32[32,5120]{1,0:T(8,128)S(1)}, f32[32,5120]{1,0:T(8,128)}, u32[]{:S(2)}) copy-start(f32[32,5120]{1,0:T(8,128)} %copy-done.1) | copy-start | bytes 1966084
  146.0 11.4 %collective-permute-start.3 = (f32[32,5120]{1,0:T(8,128)S(1)}, f32[32,5120]{1,0:T(8,128)S(1)}, u32[]{:S(2)}, u32[]{:S(2)}) collective-permute-start(f32[32,5120]{1,0:T(8,128)S(1)} %shard_map.63.refs_0_), channel_id=1, source_target_pairs={{0,1},{1,2},{2,3},{3,4},{4,5},{5,6},{6,7},{7,8},{8,9},{9,10},{10,1... | collective-permute-start | bytes 1966088 | tf_op jit(solution)/shard_map/ppermute | solution.py:146
  157.3 15.8 %collective-permute-start.5 = (f32[32,6144]{1,0:T(8,128)S(1)}, f32[32,6144]{1,0:T(8,128)S(1)}, u32[]{:S(2)}, u32[]{:S(2)}) collective-permute-start(f32[32,6144]{1,0:T(8,128)S(1)} %shard_map.65), channel_id=1, source_target_pairs={{0,1},{1,2},{2,3},{3,4},{4,5},{5,6},{6,7},{7,8},{8,9},{9,10},{10,1... | collective-permute-start | bytes 2359304 | tf_op jit(solution)/shard_map/ppermute | solution.py:146
  168.2 13.5 %collective-permute-start.4 = (f32[32,5120]{1,0:T(8,128)S(1)}, f32[32,5120]{1,0:T(8,128)S(1)}, u32[]{:S(2)}, u32[]{:S(2)}) collective-permute-start(f32[32,5120]{1,0:T(8,128)S(1)} %get-tuple-element.33), channel_id=1, source_target_pairs={{0,1},{1,2},{2,3},{3,4},{4,5},{5,6},{6,7},{7,8},{8,9},{9,10},{10,1... | collective-permute-start | bytes 1966088 | tf_op jit(solution)/shard_map/ppermute | solution.py:146
  228.1 12.2 %collective-permute-start.6 = (f32[32,5120]{1,0:T(8,128)S(1)}, f32[32,5120]{1,0:T(8,128)S(1)}, u32[]{:S(2)}, u32[]{:S(2)}) collective-permute-start(f32[32,5120]{1,0:T(8,128)S(1)} %shard_map.69.refs_0_), channel_id=1, source_target_pairs={{0,1},{1,2},{2,3},{3,4},{4,5},{5,6},{6,7},{7,8},{8,9},{9,10},{10,1... | collective-permute-start | bytes 1966088 | tf_op jit(solution)/shard_map/ppermute | solution.py:146
  240.3 15.6 %collective-permute-start.8 = (f32[32,6144]{1,0:T(8,128)S(1)}, f32[32,6144]{1,0:T(8,128)S(1)}, u32[]{:S(2)}, u32[]{:S(2)}) collective-permute-start(f32[32,6144]{1,0:T(8,128)S(1)} %shard_map.71), channel_id=1, source_target_pairs={{0,1},{1,2},{2,3},{3,4},{4,5},{5,6},{6,7},{7,8},{8,9},{9,10},{10,1... | collective-permute-start | bytes 2359304 | tf_op jit(solution)/shard_map/ppermute | solution.py:146
  251.2 13.3 %collective-permute-start.7 = (f32[32,5120]{1,0:T(8,128)S(1)}, f32[32,5120]{1,0:T(8,128)S(1)}, u32[]{:S(2)}, u32[]{:S(2)}) collective-permute-start(f32[32,5120]{1,0:T(8,128)S(1)} %get-tuple-element.37), channel_id=1, source_target_pairs={{0,1},{1,2},{2,3},{3,4},{4,5},{5,6},{6,7},{7,8},{8,9},{9,10},{10,1... | collective-permute-start | bytes 1966088 | tf_op jit(solution)/shard_map/ppermute | solution.py:146
  310.7 12.1 %collective-permute-start.9 = (f32[32,5120]{1,0:T(8,128)S(1)}, f32[32,5120]{1,0:T(8,128)S(1)}, u32[]{:S(2)}, u32[]{:S(2)}) collective-permute-start(f32[32,5120]{1,0:T(8,128)S(1)} %shard_map.75.refs_0_), channel_id=1, source_target_pairs={{0,1},{1,2},{2,3},{3,4},{4,5},{5,6},{6,7},{7,8},{8,9},{9,10},{10,1... | collective-permute-start | bytes 1966088 | tf_op jit(solution)/shard_map/ppermute | solution.py:146
  322.8 15.9 %collective-permute-start.11 = (f32[32,6144]{1,0:T(8,128)S(1)}, f32[32,6144]{1,0:T(8,128)S(1)}, u32[]{:S(2)}, u32[]{:S(2)}) collective-permute-start(f32[32,6144]{1,0:T(8,128)S(1)} %shard_map.77), channel_id=1, source_target_pairs={{0,1},{1,2},{2,3},{3,4},{4,5},{5,6},{6,7},{7,8},{8,9},{9,10},{10,1... | collective-permute-start | bytes 2359304 | tf_op jit(solution)/shard_map/ppermute | solution.py:146
  333.6 13.6 %collective-permute-start.10 = (f32[32,5120]{1,0:T(8,128)S(1)}, f32[32,5120]{1,0:T(8,128)S(1)}, u32[]{:S(2)}, u32[]{:S(2)}) collective-permute-start(f32[32,5120]{1,0:T(8,128)S(1)} %get-tuple-element.41), channel_id=1, source_target_pairs={{0,1},{1,2},{2,3},{3,4},{4,5},{5,6},{6,7},{7,8},{8,9},{9,10},{10,1... | collective-permute-start | bytes 1966088 | tf_op jit(solution)/shard_map/ppermute | solution.py:146
  393.6 12.2 %collective-permute-start.12 = (f32[32,5120]{1,0:T(8,128)S(1)}, f32[32,5120]{1,0:T(8,128)S(1)}, u32[]{:S(2)}, u32[]{:S(2)}) collective-permute-start(f32[32,5120]{1,0:T(8,128)S(1)} %shard_map.81.refs_0_), channel_id=1, source_target_pairs={{0,1},{1,2},{2,3},{3,4},{4,5},{5,6},{6,7},{7,8},{8,9},{9,10},{10,1... | collective-permute-start | bytes 1966088 | tf_op jit(solution)/shard_map/ppermute | solution.py:146
  405.8 15.6 %collective-permute-start.14 = (f32[32,6144]{1,0:T(8,128)S(1)}, f32[32,6144]{1,0:T(8,128)S(1)}, u32[]{:S(2)}, u32[]{:S(2)}) collective-permute-start(f32[32,6144]{1,0:T(8,128)S(1)} %shard_map.83), channel_id=1, source_target_pairs={{0,1},{1,2},{2,3},{3,4},{4,5},{5,6},{6,7},{7,8},{8,9},{9,10},{10,1... | collective-permute-start | bytes 2359304 | tf_op jit(solution)/shard_map/ppermute | solution.py:146
  416.7 13.3 %collective-permute-start.13 = (f32[32,5120]{1,0:T(8,128)S(1)}, f32[32,5120]{1,0:T(8,128)S(1)}, u32[]{:S(2)}, u32[]{:S(2)}) collective-permute-start(f32[32,5120]{1,0:T(8,128)S(1)} %get-tuple-element.45), channel_id=1, source_target_pairs={{0,1},{1,2},{2,3},{3,4},{4,5},{5,6},{6,7},{7,8},{8,9},{9,10},{10,1... | collective-permute-start | bytes 1966088 | tf_op jit(solution)/shard_map/ppermute | solution.py:146
  484.3 64.8 %collective-permute-start.16 = (f32[32,6144]{1,0:T(8,128)S(1)}, f32[32,6144]{1,0:T(8,128)S(1)}, u32[]{:S(2)}, u32[]{:S(2)}) collective-permute-start(f32[32,6144]{1,0:T(8,128)S(1)} %shard_map.88.refs_0_), channel_id=1, source_target_pairs={{0,11},{1,12},{2,13},{3,14},{4,15},{5,0},{6,1},{7,2},{8,3},{9,4},{... | collective-permute-start | bytes 2359304 | tf_op jit(solution)/shard_map/ppermute | solution.py:146
  491.4 50.7 %collective-permute-start.17 = (f32[32,5120]{1,0:T(8,128)S(1)}, f32[32,5120]{1,0:T(8,128)S(1)}, u32[]{:S(2)}, u32[]{:S(2)}) collective-permute-start(f32[32,5120]{1,0:T(8,128)S(1)} %shard_map.89), channel_id=1, source_target_pairs={{0,11},{1,12},{2,13},{3,14},{4,15},{5,0},{6,1},{7,2},{8,3},{9,4},{... | collective-permute-start | bytes 1966088 | tf_op jit(solution)/shard_map/ppermute | solution.py:146
  491.4 57.6 %collective-permute-start.15 = (f32[32,5120]{1,0:T(8,128)S(1)}, f32[32,5120]{1,0:T(8,128)S(1)}, u32[]{:S(2)}, u32[]{:S(2)}) collective-permute-start(f32[32,5120]{1,0:T(8,128)S(1)} %shard_map.87.refs_0_), channel_id=1, source_target_pairs={{0,11},{1,12},{2,13},{3,14},{4,15},{5,0},{6,1},{7,2},{8,3},{9,4},{... | collective-permute-start | bytes 1966088 | tf_op jit(solution)/shard_map/ppermute | solution.py:146

commit v3 on v2

--- a/solution.py
+++ b/solution.py
@@ -291,8 +291,8 @@
                 work * count,
                 moved * count,
             )(scalars, system, weighted, image, *earlier)
-            earlier = [piece]
             pieces.append(shifted(piece, "row", steps))
+            earlier = [piece] if at + 2 < len(counts) else [pieces[0]]
     return jnp.concatenate(pieces, axis=1)
 
 

time: 553 us -> 549 us (level)
  transfers between devices with their start and end apart: 18 -> 18, of which waited for: 2 -> 3; matrix products, arithmetic and copies ran while one was open for 0% -> 0% of each run, Pallas kernels for 26% -> 28%
where the time goes in v3:
time: 549 us; the launch traced here: 546 us
  Pallas kernels  423 us (77%)
  waiting for transfers between devices  53.6 us (10%)
  starting transfers between devices  39.8 us (7%)
  other arithmetic  23.6 us (4%)
    pallas_call x6, Pallas kernels, local(): called(functools.partial(middle_kernel, starts[:len(inside)]), tiles + 1,...  190 us
    pallas_call x13, Pallas kernels, local(): called(last_kernel, count, [matrix_spec(1, lambda i, start=start: start +...  97.4 us
    pallas_call x10, Pallas kernels, local(): called(functools.partial(forward_kernel, last), count, specs, weighted_sp...  81.1 us
    pallas_call x5, Pallas kernels, local(): called(crossing_kernel, count, [matrix_spec(1, lambda i, start=start: sta...  54.7 us
    ppermute x18, waiting for transfers between devices, shifted(): return lax.ppermute(value, axis, pairs)  53.6 us
    ppermute x18, starting transfers between devices, shifted(): return lax.ppermute(value, axis, pairs)  39.8 us
    reduce_sum x1, other arithmetic, local(): jnp.sum(system * system, axis=1) + epsilon  20.8 us
  transfers between devices with their start and end apart: 18, of which 3 were waited for; matrix products, arithmetic and copies ran while one was open for 0% of the time, Pallas kernels for 28%

profile of v3, /device:TPU:29, one launch (start us, length us, event | category | flops | bytes accessed | tf_op | source)
XLA Modules:
  0.0 546.3 jit_solution(9651047029760956310)
XLA Ops:
  3.3 20.8 %multiply_reduce_fusion = f32[1024]{0:T(1024)S(1)} fusion(f32[1024,16384]{1,0:T(8,128)} %matrix.25), kind=kLoop, calls=%fused_computation | loop fusion | flops 33553408 | bytes 67112960 | tf_op jit(solution)/shard_map/reduce_sum | solution.py:165
  26.5 31.4 %shard_map.56 = (f32[32,16384]{1,0:T(8,128)S(1)}, bf16[64,512]{1,0:T(8,128)(2,1)S(1)}) custom-call(s32[3]{0:T(128)S(1)} %get-tuple-element.49.scalars.refs_0_, f32[1024,16384]{1,0:T(8,128)} %matrix.25, f32[1024,16384]{1,0:T(8,128)} %matrix.25, bf16[64,512]{1,0:T(8,128)(2,1)S(1)} %shard_map.55.refs_3_, f32[2,512,512]{2,1,0:T(8,128)S(1)} %bitcast.16, ...), custom_call_target="tpu_custom_call" | custom-call | flops 16777216 | bytes 4194304 | tf_op jit(solution)/shard_map/pallas_call | solution.py:242
  65.0 8.6 %shard_map.59 = f32[32,6144]{1,0:T(8,128)} custom-call(s32[3]{0:T(128)S(1)} %get-tuple-element.49.scalars.refs_0_, f32[1024,16384]{1,0:T(8,128)} %matrix.25, bf16[64,512]{1,0:T(8,128)(2,1)S(1)} %get-tuple-element.27.weighted, f32[32,16384]{1,0:T(8,128)S(1)} %get-tuple-element.28.image, f32[32,5120]{1,0:T(8,128)S(1)} %shard_map.57.refs_0_), custom_call_target="tpu_custom_call" | custom-call | flops 3145728 | bytes 786432 | tf_op jit(solution)/shard_map/pallas_call | solution.py:279
  73.7 11.5 %shard_map.58 = (f32[32,5120]{1,0:T(8,128)}, f32[512,128]{1,0:T(8,128)S(1)}) custom-call(s32[3]{0:T(128)S(1)} %get-tuple-element.49.scalars.refs_0_, f32[1024,16384]{1,0:T(8,128)} %matrix.25, f32[1024,16384]{1,0:T(8,128)} %matrix.25, bf16[64,512]{1,0:T(8,128)(2,1)S(1)} %get-tuple-element.27.weighted, f32[32,16384]{1,0:T(8,128)S(1)} %get-tuple-element.28.image, ...), custom_call_target="tpu_custom_call" | custom-call | flops 5242880 | bytes 1310720 | tf_op jit(solution)/shard_map/pallas_call | solution.py:261
  91.0 8.6 %shard_map.60.refs_3_ = f32[512,128]{1,0:T(8,128)S(1)} custom-call(s32[3]{0:T(128)S(1)} %get-tuple-element.51.refs_0_.scalars, f32[1024,16384]{1,0:T(8,128)} %matrix.25, f32[32,6144]{1,0:T(8,128)S(1)} %collective-permute-done.2.refs_2_.refs_5_, f32[512,128]{1,0:T(8,128)S(1)} %copy-done.4), custom_call_target="tpu_custom_call" | custom-call | flops 3145728 | bytes 786432 | tf_op jit(solution)/shard_map/pallas_call | solution.py:213
  107.3 31.7 %shard_map.62 = (f32[32,16384]{1,0:T(8,128)S(1)}, bf16[64,512]{1,0:T(8,128)(2,1)S(1)}) custom-call(s32[3]{0:T(128)S(1)} %get-tuple-element.51.refs_0_.scalars, f32[1024,16384]{1,0:T(8,128)} %matrix.25, f32[1024,16384]{1,0:T(8,128)} %matrix.25, bf16[64,512]{1,0:T(8,128)(2,1)S(1)} %shard_map.61.refs_3_, f32[32,5120]{1,0:T(8,128)S(1)} %copy-done.2, ...), custom_call_target="tpu_custom_call" | custom-call | flops 16777216 | bytes 4194304 | tf_op jit(solution)/shard_map/pallas_call | solution.py:242
  149.4 7.9 %shard_map.65 = f32[32,6144]{1,0:T(8,128)S(1)} custom-call(s32[3]{0:T(128)S(1)} %get-tuple-element.51.refs_0_.scalars, f32[1024,16384]{1,0:T(8,128)} %matrix.25, bf16[64,512]{1,0:T(8,128)(2,1)S(1)} %get-tuple-element.31.weighted, f32[32,16384]{1,0:T(8,128)S(1)} %get-tuple-element.32.image, f32[32,5120]{1,0:T(8,128)S(1)} %shard_map.63.refs_0_), custom_call_target="tpu_custom_call" | custom-call | flops 3145728 | bytes 786432 | tf_op jit(solution)/shard_map/pallas_call | solution.py:279
  157.4 10.8 %shard_map.64 = (f32[32,5120]{1,0:T(8,128)S(1)}, f32[512,128]{1,0:T(8,128)S(1)}) custom-call(s32[3]{0:T(128)S(1)} %get-tuple-element.51.refs_0_.scalars, f32[1024,16384]{1,0:T(8,128)} %matrix.25, f32[1024,16384]{1,0:T(8,128)} %matrix.25, bf16[64,512]{1,0:T(8,128)(2,1)S(1)} %get-tuple-element.31.weighted, f32[32,16384]{1,0:T(8,128)S(1)} %get-tuple-element.32.image, ...), custom_call_target="tpu_custom_call" | custom-call | flops 5242880 | bytes 1310720 | tf_op jit(solution)/shard_map/pallas_call | solution.py:261
  173.1 8.6 %shard_map.66.refs_3_ = f32[512,128]{1,0:T(8,128)S(1)} custom-call(s32[3]{0:T(128)S(1)} %get-tuple-element.52.refs_0_.scalars, f32[1024,16384]{1,0:T(8,128)} %matrix.25, f32[32,6144]{1,0:T(8,128)S(1)} %collective-permute-done.5.refs_2_.refs_5_, f32[512,128]{1,0:T(8,128)S(1)} %get-tuple-element.34.refs_3_), custom_call_target="tpu_custom_call" | custom-call | flops 3145728 | bytes 786432 | tf_op jit(solution)/shard_map/pallas_call | solution.py:213
  189.4 31.7 %shard_map.68 = (f32[32,16384]{1,0:T(8,128)S(1)}, bf16[64,512]{1,0:T(8,128)(2,1)S(1)}) custom-call(s32[3]{0:T(128)S(1)} %get-tuple-element.52.refs_0_.scalars, f32[1024,16384]{1,0:T(8,128)} %matrix.25, f32[1024,16384]{1,0:T(8,128)} %matrix.25, bf16[64,512]{1,0:T(8,128)(2,1)S(1)} %shard_map.67.refs_3_, f32[32,5120]{1,0:T(8,128)S(1)} %collective-permute-done.3.arrived.refs_4_, ...), custom_call_target="tpu_custom_call" | custom-call | flops 16777216 | bytes 4194304 | tf_op jit(solution)/shard_map/pallas_call | solution.py:242
  232.3 7.9 %shard_map.71 = f32[32,6144]{1,0:T(8,128)S(1)} custom-call(s32[3]{0:T(128)S(1)} %get-tuple-element.52.refs_0_.scalars, f32[1024,16384]{1,0:T(8,128)} %matrix.25, bf16[64,512]{1,0:T(8,128)(2,1)S(1)} %get-tuple-element.35.weighted, f32[32,16384]{1,0:T(8,128)S(1)} %get-tuple-element.36.image, f32[32,5120]{1,0:T(8,128)S(1)} %shard_map.69.refs_0_), custom_call_target="tpu_custom_call" | custom-call | flops 3145728 | bytes 786432 | tf_op jit(solution)/shard_map/pallas_call | solution.py:279
  240.3 10.8 %shard_map.70 = (f32[32,5120]{1,0:T(8,128)S(1)}, f32[512,128]{1,0:T(8,128)S(1)}) custom-call(s32[3]{0:T(128)S(1)} %get-tuple-element.52.refs_0_.scalars, f32[1024,16384]{1,0:T(8,128)} %matrix.25, f32[1024,16384]{1,0:T(8,128)} %matrix.25, bf16[64,512]{1,0:T(8,128)(2,1)S(1)} %get-tuple-element.35.weighted, f32[32,16384]{1,0:T(8,128)S(1)} %get-tuple-element.36.image, ...), custom_call_target="tpu_custom_call" | custom-call | flops 5242880 | bytes 1310720 | tf_op jit(solution)/shard_map/pallas_call | solution.py:261
  255.9 8.6 %shard_map.72.refs_3_ = f32[512,128]{1,0:T(8,128)S(1)} custom-call(s32[3]{0:T(128)S(1)} %get-tuple-element.53.refs_0_.scalars, f32[1024,16384]{1,0:T(8,128)} %matrix.25, f32[32,6144]{1,0:T(8,128)S(1)} %collective-permute-done.8.refs_2_.refs_5_, f32[512,128]{1,0:T(8,128)S(1)} %get-tuple-element.38.refs_3_), custom_call_target="tpu_custom_call" | custom-call | flops 3145728 | bytes 786432 | tf_op jit(solution)/shard_map/pallas_call | solution.py:213
  272.1 31.5 %shard_map.74 = (f32[32,16384]{1,0:T(8,128)S(1)}, bf16[64,512]{1,0:T(8,128)(2,1)S(1)}) custom-call(s32[3]{0:T(128)S(1)} %get-tuple-element.53.refs_0_.scalars, f32[1024,16384]{1,0:T(8,128)} %matrix.25, f32[1024,16384]{1,0:T(8,128)} %matrix.25, bf16[64,512]{1,0:T(8,128)(2,1)S(1)} %shard_map.73.refs_3_, f32[32,5120]{1,0:T(8,128)S(1)} %collective-permute-done.6.arrived.refs_4_, ...), custom_call_target="tpu_custom_call" | custom-call | flops 16777216 | bytes 4194304 | tf_op jit(solution)/shard_map/pallas_call | solution.py:242
  322.8 10.8 %shard_map.76 = (f32[32,5120]{1,0:T(8,128)S(1)}, f32[512,128]{1,0:T(8,128)S(1)}) custom-call(s32[3]{0:T(128)S(1)} %get-tuple-element.53.refs_0_.scalars, f32[1024,16384]{1,0:T(8,128)} %matrix.25, f32[1024,16384]{1,0:T(8,128)} %matrix.25, bf16[64,512]{1,0:T(8,128)(2,1)S(1)} %get-tuple-element.39.weighted, f32[32,16384]{1,0:T(8,128)S(1)} %get-tuple-element.40.image, ...), custom_call_target="tpu_custom_call" | custom-call | flops 5242880 | bytes 1310720 | tf_op jit(solution)/shard_map/pallas_call | solution.py:261
  338.6 8.5 %shard_map.78.refs_3_ = f32[512,128]{1,0:T(8,128)S(1)} custom-call(s32[3]{0:T(128)S(1)} %get-tuple-element.54.refs_0_.scalars, f32[1024,16384]{1,0:T(8,128)} %matrix.25, f32[32,6144]{1,0:T(8,128)S(1)} %collective-permute-done.11.refs_2_.refs_5_, f32[512,128]{1,0:T(8,128)S(1)} %get-tuple-element.42.refs_3_), custom_call_target="tpu_custom_call" | custom-call | flops 3145728 | bytes 786432 | tf_op jit(solution)/shard_map/pallas_call | solution.py:213
  354.9 31.7 %shard_map.80 = (f32[32,16384]{1,0:T(8,128)S(1)}, bf16[64,512]{1,0:T(8,128)(2,1)S(1)}) custom-call(s32[3]{0:T(128)S(1)} %get-tuple-element.54.refs_0_.scalars, f32[1024,16384]{1,0:T(8,128)} %matrix.25, f32[1024,16384]{1,0:T(8,128)} %matrix.25, bf16[64,512]{1,0:T(8,128)(2,1)S(1)} %shard_map.79.refs_3_, f32[32,5120]{1,0:T(8,128)S(1)} %collective-permute-done.9.arrived.refs_4_, ...), custom_call_target="tpu_custom_call" | custom-call | flops 16777216 | bytes 4194304 | tf_op jit(solution)/shard_map/pallas_call | solution.py:242
  397.8 7.9 %shard_map.83 = f32[32,6144]{1,0:T(8,128)S(1)} custom-call(s32[3]{0:T(128)S(1)} %get-tuple-element.54.refs_0_.scalars, f32[1024,16384]{1,0:T(8,128)} %matrix.25, bf16[64,512]{1,0:T(8,128)(2,1)S(1)} %get-tuple-element.43.weighted, f32[32,16384]{1,0:T(8,128)S(1)} %get-tuple-element.44.image, f32[32,5120]{1,0:T(8,128)S(1)} %shard_map.81.refs_0_), custom_call_target="tpu_custom_call" | custom-call | flops 3145728 | bytes 786432 | tf_op jit(solution)/shard_map/pallas_call | solution.py:279
  405.9 10.8 %shard_map.82 = (f32[32,5120]{1,0:T(8,128)S(1)}, f32[512,128]{1,0:T(8,128)S(1)}) custom-call(s32[3]{0:T(128)S(1)} %get-tuple-element.54.refs_0_.scalars, f32[1024,16384]{1,0:T(8,128)} %matrix.25, f32[1024,16384]{1,0:T(8,128)} %matrix.25, bf16[64,512]{1,0:T(8,128)(2,1)S(1)} %get-tuple-element.43.weighted, f32[32,16384]{1,0:T(8,128)S(1)} %get-tuple-element.44.image, ...), custom_call_target="tpu_custom_call" | custom-call | flops 5242880 | bytes 1310720 | tf_op jit(solution)/shard_map/pallas_call | solution.py:261
  421.4 8.6 %shard_map.84.refs_3_ = f32[512,128]{1,0:T(8,128)S(1)} custom-call(s32[3]{0:T(128)S(1)} %get-tuple-element.55.refs_0_.scalars, f32[1024,16384]{1,0:T(8,128)} %matrix.25, f32[32,6144]{1,0:T(8,128)S(1)} %collective-permute-done.14.refs_2_.refs_5_, f32[512,128]{1,0:T(8,128)S(1)} %get-tuple-element.46.refs_3_), custom_call_target="tpu_custom_call" | custom-call | flops 3145728 | bytes 786432 | tf_op jit(solution)/shard_map/pallas_call | solution.py:213
  437.6 31.5 %shard_map.86 = (f32[32,16384]{1,0:T(8,128)S(1)}, bf16[64,512]{1,0:T(8,128)(2,1)S(1)}) custom-call(s32[3]{0:T(128)S(1)} %get-tuple-element.55.refs_0_.scalars, f32[1024,16384]{1,0:T(8,128)} %matrix.25, f32[1024,16384]{1,0:T(8,128)} %matrix.25, bf16[64,512]{1,0:T(8,128)(2,1)S(1)} %shard_map.85.refs_3_, ...), custom_call_target="tpu_custom_call" | custom-call | flops 16777216 | bytes 4194304 | tf_op jit(solution)/shard_map/pallas_call | solution.py:242
  476.2 7.9 %shard_map.88 = f32[32,6144]{1,0:T(8,128)S(1)} custom-call(s32[3]{0:T(128)S(1)} %get-tuple-element.55.refs_0_.scalars, f32[1024,16384]{1,0:T(8,128)} %matrix.25, bf16[64,512]{1,0:T(8,128)(2,1)S(1)} %get-tuple-element.47.weighted, f32[32,16384]{1,0:T(8,128)S(1)} %get-tuple-element.48.image, f32[32,5120]{1,0:T(8,128)S(1)} %shard_map.87.refs_0_), custom_call_target="tpu_custom_call" | custom-call | flops 3145728 | bytes 786432 | tf_op jit(solution)/shard_map/pallas_call | solution.py:279
  484.2 41.8 %collective-permute-done.15.refs_0_ = f32[32,5120]{1,0:T(8,128)S(1)} collective-permute-done((f32[32,5120]{1,0:T(8,128)S(1)}, f32[32,5120]{1,0:T(8,128)S(1)}, u32[]{:S(2)}, u32[]{:S(2)}) %collective-permute-start.15) | collective-permute-done | bytes 655392 | tf_op jit(solution)/shard_map/ppermute | solution.py:146
  534.4 10.5 %collective-permute-done.17 = f32[32,5120]{1,0:T(8,128)S(1)} collective-permute-done((f32[32,5120]{1,0:T(8,128)S(1)}, f32[32,5120]{1,0:T(8,128)S(1)}, u32[]{:S(2)}, u32[]{:S(2)}) %collective-permute-start.17) | collective-permute-done | bytes 655392 | tf_op jit(solution)/shard_map/ppermute | solution.py:146
  (67 shorter events, 145.5 us)
Async XLA Ops:
  0.0 24.1 %copy-start = (f32[8]{0:T(128)S(1)}, f32[8]{0:T(128)}, u32[]{:S(2)}) copy-start(f32[8]{0:T(128)} %param.8) | copy-start | bytes 100
  3.3 20.8 %copy-start.5 = (s32[1024]{0:T(1024)S(1)}, s32[1024]{0:T(1024)}, u32[]{:S(2)}) copy-start(s32[1024]{0:T(1024)} %param.7) | copy-start | bytes 12292
  65.0 8.7 %collective-permute-start = (f32[32,5120]{1,0:T(8,128)S(1)}, f32[32,5120]{1,0:T(8,128)S(1)}, u32[]{:S(2)}, u32[]{:S(2)}) collective-permute-start(f32[32,5120]{1,0:T(8,128)S(1)} %shard_map.57.refs_0_), channel_id=1, source_target_pairs={{0,1},{1,2},{2,3},{3,4},{4,5},{5,6},{6,7},{7,8},{8,9},{9,10},{10,1... | collective-permute-start | bytes 1966088 | tf_op jit(solution)/shard_map/ppermute | solution.py:146
  73.7 16.4 %collective-permute-start.2 = (f32[32,6144]{1,0:T(8,128)}, f32[32,6144]{1,0:T(8,128)S(1)}, u32[]{:S(2)}, u32[]{:S(2)}) collective-permute-start(f32[32,6144]{1,0:T(8,128)} %shard_map.59), channel_id=1, source_target_pairs={{0,1},{1,2},{2,3},{3,4},{4,5},{5,6},{6,7},{7,8},{8,9},{9,10},{10,1... | collective-permute-start | bytes 2359304 | tf_op jit(solution)/shard_map/ppermute | solution.py:146
  73.7 11.5 %copy-start.1 = (f32[32,5120]{1,0:T(8,128)}, f32[32,5120]{1,0:T(8,128)S(1)}, u32[]{:S(2)}) copy-start(f32[32,5120]{1,0:T(8,128)S(1)} %collective-permute-done.arrived.refs_4_) | copy-start | bytes 1966084
  85.2 0.7 copy-start.3
  85.9 13.6 %collective-permute-start.1 = (f32[32,5120]{1,0:T(8,128)}, f32[32,5120]{1,0:T(8,128)S(1)}, u32[]{:S(2)}, u32[]{:S(2)}) collective-permute-start(f32[32,5120]{1,0:T(8,128)} %get-tuple-element.29), channel_id=1, source_target_pairs={{0,1},{1,2},{2,3},{3,4},{4,5},{5,6},{6,7},{7,8},{8,9},{9,10},{10,1... | collective-permute-start | bytes 1966088 | tf_op jit(solution)/shard_map/ppermute | solution.py:146
  90.0 1.0 copy-start.4
  99.6 7.7 %copy-start.2 = (f32[32,5120]{1,0:T(8,128)S(1)}, f32[32,5120]{1,0:T(8,128)}, u32[]{:S(2)}) copy-start(f32[32,5120]{1,0:T(8,128)} %copy-done.1) | copy-start | bytes 1966084
  146.0 11.4 %collective-permute-start.3 = (f32[32,5120]{1,0:T(8,128)S(1)}, f32[32,5120]{1,0:T(8,128)S(1)}, u32[]{:S(2)}, u32[]{:S(2)}) collective-permute-start(f32[32,5120]{1,0:T(8,128)S(1)} %shard_map.63.refs_0_), channel_id=1, source_target_pairs={{0,1},{1,2},{2,3},{3,4},{4,5},{5,6},{6,7},{7,8},{8,9},{9,10},{10,1... | collective-permute-start | bytes 1966088 | tf_op jit(solution)/shard_map/ppermute | solution.py:146
  157.3 15.8 %collective-permute-start.5 = (f32[32,6144]{1,0:T(8,128)S(1)}, f32[32,6144]{1,0:T(8,128)S(1)}, u32[]{:S(2)}, u32[]{:S(2)}) collective-permute-start(f32[32,6144]{1,0:T(8,128)S(1)} %shard_map.65), channel_id=1, source_target_pairs={{0,1},{1,2},{2,3},{3,4},{4,5},{5,6},{6,7},{7,8},{8,9},{9,10},{10,1... | collective-permute-start | bytes 2359304 | tf_op jit(solution)/shard_map/ppermute | solution.py:146
  168.2 13.5 %collective-permute-start.4 = (f32[32,5120]{1,0:T(8,128)S(1)}, f32[32,5120]{1,0:T(8,128)S(1)}, u32[]{:S(2)}, u32[]{:S(2)}) collective-permute-start(f32[32,5120]{1,0:T(8,128)S(1)} %get-tuple-element.33), channel_id=1, source_target_pairs={{0,1},{1,2},{2,3},{3,4},{4,5},{5,6},{6,7},{7,8},{8,9},{9,10},{10,1... | collective-permute-start | bytes 1966088 | tf_op jit(solution)/shard_map/ppermute | solution.py:146
  228.1 12.2 %collective-permute-start.6 = (f32[32,5120]{1,0:T(8,128)S(1)}, f32[32,5120]{1,0:T(8,128)S(1)}, u32[]{:S(2)}, u32[]{:S(2)}) collective-permute-start(f32[32,5120]{1,0:T(8,128)S(1)} %shard_map.69.refs_0_), channel_id=1, source_target_pairs={{0,1},{1,2},{2,3},{3,4},{4,5},{5,6},{6,7},{7,8},{8,9},{9,10},{10,1... | collective-permute-start | bytes 1966088 | tf_op jit(solution)/shard_map/ppermute | solution.py:146
  240.3 15.6 %collective-permute-start.8 = (f32[32,6144]{1,0:T(8,128)S(1)}, f32[32,6144]{1,0:T(8,128)S(1)}, u32[]{:S(2)}, u32[]{:S(2)}) collective-permute-start(f32[32,6144]{1,0:T(8,128)S(1)} %shard_map.71), channel_id=1, source_target_pairs={{0,1},{1,2},{2,3},{3,4},{4,5},{5,6},{6,7},{7,8},{8,9},{9,10},{10,1... | collective-permute-start | bytes 2359304 | tf_op jit(solution)/shard_map/ppermute | solution.py:146
  251.2 13.3 %collective-permute-start.7 = (f32[32,5120]{1,0:T(8,128)S(1)}, f32[32,5120]{1,0:T(8,128)S(1)}, u32[]{:S(2)}, u32[]{:S(2)}) collective-permute-start(f32[32,5120]{1,0:T(8,128)S(1)} %get-tuple-element.37), channel_id=1, source_target_pairs={{0,1},{1,2},{2,3},{3,4},{4,5},{5,6},{6,7},{7,8},{8,9},{9,10},{10,1... | collective-permute-start | bytes 1966088 | tf_op jit(solution)/shard_map/ppermute | solution.py:146
  310.7 12.1 %collective-permute-start.9 = (f32[32,5120]{1,0:T(8,128)S(1)}, f32[32,5120]{1,0:T(8,128)S(1)}, u32[]{:S(2)}, u32[]{:S(2)}) collective-permute-start(f32[32,5120]{1,0:T(8,128)S(1)} %shard_map.75.refs_0_), channel_id=1, source_target_pairs={{0,1},{1,2},{2,3},{3,4},{4,5},{5,6},{6,7},{7,8},{8,9},{9,10},{10,1... | collective-permute-start | bytes 1966088 | tf_op jit(solution)/shard_map/ppermute | solution.py:146
  322.8 15.9 %collective-permute-start.11 = (f32[32,6144]{1,0:T(8,128)S(1)}, f32[32,6144]{1,0:T(8,128)S(1)}, u32[]{:S(2)}, u32[]{:S(2)}) collective-permute-start(f32[32,6144]{1,0:T(8,128)S(1)} %shard_map.77), channel_id=1, source_target_pairs={{0,1},{1,2},{2,3},{3,4},{4,5},{5,6},{6,7},{7,8},{8,9},{9,10},{10,1... | collective-permute-start | bytes 2359304 | tf_op jit(solution)/shard_map/ppermute | solution.py:146
  333.6 13.6 %collective-permute-start.10 = (f32[32,5120]{1,0:T(8,128)S(1)}, f32[32,5120]{1,0:T(8,128)S(1)}, u32[]{:S(2)}, u32[]{:S(2)}) collective-permute-start(f32[32,5120]{1,0:T(8,128)S(1)} %get-tuple-element.41), channel_id=1, source_target_pairs={{0,1},{1,2},{2,3},{3,4},{4,5},{5,6},{6,7},{7,8},{8,9},{9,10},{10,1... | collective-permute-start | bytes 1966088 | tf_op jit(solution)/shard_map/ppermute | solution.py:146
  393.6 12.2 %collective-permute-start.12 = (f32[32,5120]{1,0:T(8,128)S(1)}, f32[32,5120]{1,0:T(8,128)S(1)}, u32[]{:S(2)}, u32[]{:S(2)}) collective-permute-start(f32[32,5120]{1,0:T(8,128)S(1)} %shard_map.81.refs_0_), channel_id=1, source_target_pairs={{0,1},{1,2},{2,3},{3,4},{4,5},{5,6},{6,7},{7,8},{8,9},{9,10},{10,1... | collective-permute-start | bytes 1966088 | tf_op jit(solution)/shard_map/ppermute | solution.py:146
  405.8 15.6 %collective-permute-start.14 = (f32[32,6144]{1,0:T(8,128)S(1)}, f32[32,6144]{1,0:T(8,128)S(1)}, u32[]{:S(2)}, u32[]{:S(2)}) collective-permute-start(f32[32,6144]{1,0:T(8,128)S(1)} %shard_map.83), channel_id=1, source_target_pairs={{0,1},{1,2},{2,3},{3,4},{4,5},{5,6},{6,7},{7,8},{8,9},{9,10},{10,1... | collective-permute-start | bytes 2359304 | tf_op jit(solution)/shard_map/ppermute | solution.py:146
  416.6 13.3 %collective-permute-start.13 = (f32[32,5120]{1,0:T(8,128)S(1)}, f32[32,5120]{1,0:T(8,128)S(1)}, u32[]{:S(2)}, u32[]{:S(2)}) collective-permute-start(f32[32,5120]{1,0:T(8,128)S(1)} %get-tuple-element.45), channel_id=1, source_target_pairs={{0,1},{1,2},{2,3},{3,4},{4,5},{5,6},{6,7},{7,8},{8,9},{9,10},{10,1... | collective-permute-start | bytes 1966088 | tf_op jit(solution)/shard_map/ppermute | solution.py:146
  476.2 49.8 %collective-permute-start.15 = (f32[32,5120]{1,0:T(8,128)S(1)}, f32[32,5120]{1,0:T(8,128)S(1)}, u32[]{:S(2)}, u32[]{:S(2)}) collective-permute-start(f32[32,5120]{1,0:T(8,128)S(1)} %shard_map.87.refs_0_), channel_id=1, source_target_pairs={{0,11},{1,12},{2,13},{3,14},{4,15},{5,0},{6,1},{7,2},{8,3},{9,4},{... | collective-permute-start | bytes 1966088 | tf_op jit(solution)/shard_map/ppermute | solution.py:146
  484.1 50.2 %collective-permute-start.16 = (f32[32,6144]{1,0:T(8,128)S(1)}, f32[32,6144]{1,0:T(8,128)S(1)}, u32[]{:S(2)}, u32[]{:S(2)}) collective-permute-start(f32[32,6144]{1,0:T(8,128)S(1)} %shard_map.88), channel_id=1, source_target_pairs={{0,11},{1,12},{2,13},{3,14},{4,15},{5,0},{6,1},{7,2},{8,3},{9,4},{... | collective-permute-start | bytes 2359304 | tf_op jit(solution)/shard_map/ppermute | solution.py:146
  533.0 11.9 %collective-permute-start.17 = (f32[32,5120]{1,0:T(8,128)S(1)}, f32[32,5120]{1,0:T(8,128)S(1)}, u32[]{:S(2)}, u32[]{:S(2)}) collective-permute-start(f32[32,5120]{1,0:T(8,128)S(1)} %shard_map.89), channel_id=1, source_target_pairs={{0,11},{1,12},{2,13},{3,14},{4,15},{5,0},{6,1},{7,2},{8,3},{9,4},{... | collective-permute-start | bytes 1966088 | tf_op jit(solution)/shard_map/ppermute | solution.py:146
